TPU v7x, 32 devices: a whole 2x2x4 slice. The times are simulated.
32 devices in a mesh: groups: 2 (over y), tiles: 4 (over z), folds: 2 (over x), sub: 2 (over core).
Axes of the slice: x: 2, y: 2, z: 4, core: 2. Of those that a mesh axis runs over, the one named last changes fastest.
Arguments:
- features: bfloat16 [2, 32, 16, 16, 1024], P('folds', ('groups', 'tiles', 'sub')), parts along dimension 1, may hold values from -6 to 6
- conv_first: bfloat16 [2, 3, 3, 3, 64, 32], P('folds'), may hold values from -0.15625 to 0.15625
- gain_first: float32 [2, 32], P('folds'), may hold values from 0.1 to 1.9
- shift_first: float32 [2, 32], P('folds'), may hold values from -3 to 3
- conv_second: bfloat16 [2, 3, 3, 3, 32, 32], P('folds'), may hold values from -0.21875 to 0.21875
- gain_second: float32 [2, 32], P('folds'), may hold values from 0.1 to 1.9
- shift_second: float32 [2, 32], P('folds'), may hold values from -3 to 3
- head_weight: bfloat16 [2, 32, 16], P('folds'), may hold values from -1 to 1
- head_bias: float32 [2, 16], P('folds'), may hold values from -4 to 4
- corners: int32 [32, 3], P(('groups', 'tiles', 'sub')), parts along dimension 0, may hold values from 0 to 48, as said below
- counts: int32 [8, 2], P('groups'), parts along dimension 0, may hold values from 0 to 2, as said below
Outputs:
- logits: float32 [128, 40, 640], P(('groups', 'tiles'), ('folds', 'sub')), parts along dimension 0
There are 2 independent parts, one for each index of `groups`. A program takes and returns all parts, laid end to end along the dimension named above; an argument that names none is the same for every part. Nothing has to cross between parts.
Inputs may be any that keep to these rules, and one draw needn't show every extreme that they name: `corners`: for slot n = (t * 2 + s) * 2 + j, the z coordinate lies in [t * 16, (t + 1) * 16) and equals (3) * 16 in the last slab; x lies in [0, 24] and y in [0, 24]. counts[t, s] + counts[t xor (2), s] <= 2 for every t and s; some entry equals 2.
All inputs are finite; a program needn't handle non-finite values.
Results may differ from a plain program's by a relative error of at most 0.01.
Values may be sent and summed in bfloat16 or wider, within the bound.
No kernel may reach another device: no remote copies, remote signals or barrier semaphores. Data moves between devices by JAX's collectives and lax.ppermute only.
A program may use at most 128 MiB of HBM per device.

v0:
```python
import functools

import jax
import jax.numpy as jnp
from jax import lax
from jax.experimental import pallas as pl
from jax.experimental.pallas import tpu as pltpu
from jax.sharding import PartitionSpec as P

TZ = 16
VX = 40
VY = 40

epsilon = 1e-05
leak_slope = 0.01
far = 1 << 20
bf16 = jnp.bfloat16
f32 = jnp.float32
vmem_bytes = 48 << 20


def iota(shape, dim):
    return lax.broadcasted_iota(jnp.int32, shape, dim)


def tile_matrix(width, lanes):
    return (iota((width, lanes), 1) % width == iota((width, lanes), 0)).astype(bf16)


def tiled_row(ref, lanes):
    width = ref.shape[1]
    row = jnp.concatenate([ref[...], jnp.zeros((1, lanes - width), f32)], axis=1)
    row = jnp.broadcast_to(row, (8, lanes))
    reach = width
    while reach < lanes:
        row = row + pltpu.roll(row, reach, 1)
        reach *= 2
    return row[0:1]


def lane_bands(parts, places):
    total = None
    for place, part in enumerate(parts):
        if part is not None:
            total = part if total is None else jnp.where(places == place, part, total)
    if total is None:
        return None
    if any(part is None for part in parts):
        empty = None
        for place, part in enumerate(parts):
            if part is None:
                here = places == place
                empty = here if empty is None else empty | here
        total = jnp.where(empty, 0.0, total)
    return total


def build_pairs(taps_ref, band_ref, in_width, width, swapped, dz):
    spread = tile_matrix(width, 128)
    places = iota((in_width, 128), 1) // width
    zero = jnp.zeros((in_width, 128), bf16)
    orders = (((1, 0), (2, None)), ((0, 1), (None, 2)))
    tiled = {}
    if swapped:
        for tap in range(9):
            at = (dz * 9 + tap) * width
            tiled[divmod(tap, 3)] = lax.dot_general(
                taps_ref[at : at + width],
                spread,
                (((0,), (0,)), ((), ())),
                preferred_element_type=f32,
            )
    else:
        at = dz * 9 * in_width
        wide = jnp.dot(taps_ref[at : at + 9 * in_width], spread, preferred_element_type=f32)
        for tap in range(9):
            tiled[divmod(tap, 3)] = wide[tap * in_width : (tap + 1) * in_width]
    for variant in range(2):
        for yi in range(4):
            for side in range(2):
                parts = []
                for dx in orders[variant][side]:
                    for yo in range(2):
                        parts.append(None if dx is None else tiled.get((dx, yi - yo)))
                block = lane_bands(parts, places)
                at = (dz * 4 + yi) * in_width
                band_ref[variant, at : at + in_width, side * 128 : (side + 1) * 128] = (
                    zero if block is None else block.astype(bf16)
                )


def banded(pad_ref, lane, count, edge, band):
    depth = band.shape[0] // 3
    view = [pad_ref[dz * edge : dz * edge + count, lane : lane + depth] for dz in range(3)]
    return jnp.dot(jnp.concatenate(view, axis=1), band, preferred_element_type=f32)


def join_pair(even, odd, low, across, edge):
    if odd is None:
        here = jnp.where(low, even[:, :128], 0.0)
        before = jnp.where(low, 0.0, even[:, :128])
        after = even[:, 128:]
    else:
        here = jnp.where(low, even[:, :128], odd[:, :128])
        before = jnp.where(low, odd[:, :128], even[:, :128])
        after = even[:, 128:] + odd[:, 128:]
    return join_across(pltpu.roll(before, 64, 1), here, after, across, edge)


def join_across(before, here, after, across, edge):
    rows = here.shape[0]
    before = jnp.where(across == 0, 0.0, pltpu.roll(before, 1, 0))
    after = jnp.where(across == edge - 1, 0.0, pltpu.roll(after, rows - 1, 0))
    return here + before + after


def folded(row, width):
    row = jnp.broadcast_to(row, (8, 128))
    reach = width
    while reach < 128:
        row = row + pltpu.roll(row, reach, 1)
        reach *= 2
    return row[0:1]


class Norm:
    def __init__(self, width, rows, voxels):
        self.width, self.rows, self.voxels = width, rows, voxels
        self.base = None
        self.first = self.second = 0.0

    def take(self, block, mask, held):
        kept = block if mask is None else jnp.where(mask, block, 0.0)
        if self.base is None:
            total = folded(jnp.sum(kept, axis=0, keepdims=True), self.width)
            self.base = total * (1.0 / (self.rows * held))
        moved = block - self.base
        if mask is not None:
            moved = jnp.where(mask, moved, 0.0)
        self.first = self.first + jnp.sum(moved, axis=0, keepdims=True)
        self.second = self.second + jnp.sum(moved * moved, axis=0, keepdims=True)

    def settle(self, gain, shift):
        off = folded(self.first, self.width) * (1.0 / self.voxels)
        variance = folded(self.second, self.width) * (1.0 / self.voxels) - off * off
        self.center = self.base + off
        self.factor = lax.rsqrt(jnp.maximum(variance, 0.0) + epsilon) * gain
        self.shift = shift

    def give(self, block, mask):
        scaled = (block - self.center) * self.factor + self.shift
        scaled = jnp.maximum(scaled, leak_slope * scaled)
        return scaled if mask is None else jnp.where(mask, scaled, 0.0)


def section_kernel(
    sizes,
    corners_hbm,
    counts_hbm,
    features_ref,
    taps_one_hbm,
    gain_one_hbm,
    shift_one_hbm,
    taps_two_hbm,
    gain_two_hbm,
    shift_two_hbm,
    head_hbm,
    bias_hbm,
    *rest,
):
    slots, edge, chunk, parts = sizes
    out_refs = rest[: len(parts)]
    (
        pad_one,
        pad_two,
        pad_turned,
        band_one,
        band_two,
        hidden,
        outcome,
        corners_ref,
        counts_ref,
        taps_one_ref,
        gain_one_ref,
        shift_one_ref,
        taps_two_ref,
        gain_two_ref,
        shift_two_ref,
        head_ref,
        bias_ref,
        selects,
        sems,
    ) = rest[len(parts) :]
    in_width = taps_one_ref.shape[1]
    classes, width = head_ref.shape
    area = edge * edge
    stride = area + edge
    count = hidden.shape[0]
    voxels = float(area * edge)
    data = edge * in_width
    lanes = edge * classes

    copies = []
    for at, (source, target) in enumerate(
        [
            (taps_one_hbm, taps_one_ref),
            (taps_two_hbm, taps_two_ref),
            (gain_one_hbm, gain_one_ref),
            (shift_one_hbm, shift_one_ref),
            (gain_two_hbm, gain_two_ref),
            (shift_two_hbm, shift_two_ref),
            (head_hbm, head_ref),
            (bias_hbm, bias_ref),
            (corners_hbm, corners_ref),
            (counts_hbm, counts_ref),
        ]
        + [
            (
                features_ref.at[slot],
                pad_one.at[pl.ds(edge + slot * stride, area), pl.ds(128, data)],
            )
            for slot in range(slots)
        ]
    ):
        copy = pltpu.make_async_copy(source, target, sems.at[at])
        copy.start()
        copies.append(copy)
    for pad in (pad_one, pad_two, pad_turned):
        for slot in range(slots + 1):
            pad[slot * stride : slot * stride + edge, :] = jnp.zeros((edge, pad.shape[1]), bf16)
    pad_one[:, :128] = jnp.zeros((pad_one.shape[0], 128), bf16)
    pad_one[:, 128 + data :] = jnp.zeros((pad_one.shape[0], 128), bf16)

    center, spread = (edge - 1) / 2.0, edge / 4.0

    def profile(offset):
        return jnp.exp(-((offset.astype(f32) - center) ** 2) / (2.0 * spread * spread))

    row_at = iota((area, 128), 0)
    lane_at = iota((1, lanes), 1)
    gauss = profile(row_at // edge) * profile(row_at % edge)
    gauss = jnp.concatenate([gauss] * (lanes // 128), axis=1) * profile(lane_at // classes)

    row = iota((chunk * edge, area), 0)
    source = iota((chunk * edge, area), 1)
    turn = (row % edge - source // edge) & (edge - 1)
    code = turn + edge * (source % edge - row // edge)
    across = iota((count, 128), 0) % edge
    tile_index = lax.axis_index("tiles")
    sub_index = lax.axis_index("sub")
    position = lax.axis_index("folds") * lax.axis_size("sub") + sub_index

    for copy in copies[:-slots]:
        copy.wait()
    for dz in range(3):
        build_pairs(taps_one_ref, band_one, in_width, width, True, dz)
    gain_one, shift_one = tiled_row(gain_one_ref, 128), tiled_row(shift_one_ref, 128)
    gain_two, shift_two = tiled_row(gain_two_ref, 128), tiled_row(shift_two_ref, 128)

    half = edge // 2
    head_row = lax.dot_general(
        head_ref[...],
        tile_matrix(classes, half * classes),
        (((0,), (0,)), ((), ())),
        preferred_element_type=f32,
    )
    block = (half * width, half * classes)
    head_block = jnp.where(
        iota(block, 0) // width == iota(block, 1) // classes,
        jnp.concatenate([head_row] * half, axis=0),
        0.0,
    ).astype(bf16)
    bias = tiled_row(bias_ref, lanes)

    mark = iota((edge, lanes), 0)
    notes = jnp.zeros((edge, lanes), f32)
    for slot in range(slots):
        depth = corners_ref[slot, 0] - tile_index * TZ
        notes = jnp.where(mark == 2 * slot, depth.astype(f32), notes)
        notes = jnp.where(mark == 2 * slot + 1, corners_ref[slot, 2].astype(f32), notes)
    for (_, low_row, high_row, noted), out_ref in zip(parts, out_refs):
        if noted:
            out_ref[slots * edge * (high_row - low_row) :, :] = notes.astype(bf16)

    for copy in copies[-slots:]:
        copy.wait()
    low = iota((count, 128), 1) < 64
    spot = iota((area, 128), 1)
    pairs = edge // 4 + 1
    masks = [None] * pairs
    masks[0] = spot >= width
    masks[-1] = spot < width
    norms = [Norm(width, area, voxels) for _ in range(slots)]
    for pair in range(pairs):
        even = banded(pad_one, 256 * pair, count, edge, band_one[0])
        odd = None
        if pair < pairs - 1:
            odd = banded(pad_one, 256 * pair + 128, count, edge, band_one[1])
        block = join_pair(even, odd, low, across, edge)
        hidden[:, pair * 128 : (pair + 1) * 128] = block
        for slot, norm in enumerate(norms):
            norm.take(block[slot * stride : slot * stride + area], masks[pair], 3)
        if pair < 3:
            build_pairs(taps_two_ref, band_two, width, width, False, pair)
    for norm in norms:
        norm.settle(gain_one, shift_one)

    fresh = {}
    near = spot < 64

    def refresh(pair):
        for slot, norm in enumerate(norms):
            at = slot * stride
            block = norm.give(hidden[at : at + area, pair * 128 : (pair + 1) * 128], masks[pair])
            rows_at = pl.ds(at + edge, area)
            pad_two[rows_at, pair * 128 : (pair + 1) * 128] = block.astype(bf16)
            if pair > 0:
                turned = pltpu.roll(jnp.where(near, block, fresh[slot]), 64, 1)
                pad_turned[rows_at, (pair - 1) * 128 : pair * 128] = turned.astype(bf16)
            fresh[slot] = block

    def prepare(slot):
        depth = corners_ref[slot, 0] - tile_index * TZ
        alive = slot < counts_ref[sub_index, tile_index]
        start = 0
        for peer, low_row, high_row, _ in parts:
            wanted = depth + edge * ((position ^ peer) * chunk - corners_ref[slot, 1])
            wanted = jnp.where(alive, wanted, far)
            select = (code[low_row * edge : high_row * edge] == wanted).astype(f32).astype(bf16)
            selects[slot, start : start + select.shape[0], :] = select
            start += select.shape[0]

    quads = edge // 4
    seconds = [Norm(width, area, voxels) for _ in range(slots)]
    refresh(0)
    for quad in range(quads):
        refresh(quad + 1)
        even = banded(pad_two, 128 * quad, count, edge, band_two[0])
        odd = banded(pad_turned, 128 * quad, count, edge, band_two[1])
        block = join_pair(even, odd, low, across, edge)
        outcome[:, quad * 128 : (quad + 1) * 128] = block
        for slot, norm in enumerate(seconds):
            norm.take(block[slot * stride : slot * stride + area], None, 4)
        if quad < slots:
            prepare(quad)
    for slot in range(quads, slots):
        prepare(slot)
    for norm in seconds:
        norm.settle(gain_two, shift_two)

    for slot, norm in enumerate(seconds):
        at = slot * stride
        logits = []
        for side in range(2):
            normed = [
                norm.give(outcome[at : at + area, quad * 128 : (quad + 1) * 128], None).astype(
                    bf16
                )
                for quad in range(side * quads // 2, (side + 1) * quads // 2)
            ]
            logits.append(
                jnp.dot(
                    jnp.concatenate(normed, axis=1), head_block, preferred_element_type=f32
                )
            )
        weighted = (jnp.concatenate(logits, axis=1) + bias) * gauss
        lane_start = corners_ref[slot, 2] * classes
        weighted = pltpu.roll(weighted, lane_start % lanes, 1).astype(bf16)
        placed = jnp.dot(selects[slot], weighted, preferred_element_type=f32).astype(bf16)
        start = 0
        for (_, low_row, high_row, _), out_ref in zip(parts, out_refs):
            size = (high_row - low_row) * edge
            out_ref[slot * size : (slot + 1) * size, :] = placed[start : start + size]
            start += size


def gather_kernel(sizes, spilled, *rest):
    slots, edge, chunk, parts, first, last, classes = sizes
    part_refs = rest[: len(parts)]
    out_ref = rest[len(parts)]
    lanes = edge * classes
    blocks = -(-VY * classes // lanes)

    depth_at = iota((edge, lanes), 0)
    lane_at = iota((edge, lanes), 1)
    groups = []
    for (peer, low_row, high_row, noted), part_ref in zip(parts, part_refs):
        if not noted or any(group[0] == peer % 2 for group in groups):
            continue
        notes = part_ref[slots * edge * (high_row - low_row) :, :].astype(f32).astype(jnp.int32)
        for slot in range(slots):
            depth = notes[2 * slot : 2 * slot + 1]
            start = notes[2 * slot + 1 : 2 * slot + 2] * classes
            keep = depth_at < depth if spilled else depth_at >= depth
            inside = []
            for block in range(blocks):
                lane = lane_at + block * lanes
                inside.append(keep & (lane >= start) & (lane < start + lanes))
            groups.append((peer % 2, slot, inside))

    for across in range(first, last):
        total = [jnp.zeros((edge, lanes), f32) for _ in range(blocks)]
        for parity, slot, inside in groups:
            piece = None
            for (peer, low_row, high_row, _), part_ref in zip(parts, part_refs):
                if peer % 2 == parity and low_row <= across < high_row:
                    at = (slot * (high_row - low_row) + across - low_row) * edge
                    part = part_ref[at : at + edge, :].astype(f32)
                    piece = part if piece is None else piece + part
            for block in range(blocks):
                total[block] = total[block] + jnp.where(inside[block], piece, 0.0)
        total = jnp.concatenate(total, axis=1)[:, : VY * classes]
        out_ref[across - first] = total.astype(out_ref.dtype)


def join_kernel(low_row, own_ref, odd_ref, even_ref, *rest):
    out_ref, total, sems = rest[-3:]
    tile_index = lax.axis_index("tiles")
    from_even = (tile_index % 2 == 1).astype(f32)
    from_odd = ((tile_index % 2 == 0) & (tile_index > 0)).astype(f32)
    copies = []
    for row in range(even_ref.shape[0]):
        total[row] = (
            own_ref[low_row + row]
            + even_ref[row].astype(f32) * from_even
            + odd_ref[row].astype(f32) * from_odd
        )
        copy = pltpu.make_async_copy(total.at[row], out_ref.at[low_row + row], sems.at[row])
        copy.start()
        copies.append(copy)
    for copy in copies:
        copy.wait()


vmem = pl.BlockSpec(memory_space=pltpu.VMEM)
hbm = pl.BlockSpec(memory_space=pltpu.HBM)
limits = pltpu.CompilerParams(vmem_limit_bytes=vmem_bytes)
ample = pltpu.CompilerParams(vmem_limit_bytes=60000000)


def on_device(
    features,
    conv_first,
    gain_first,
    shift_first,
    conv_second,
    gain_second,
    shift_second,
    head_weight,
    head_bias,
    corners,
    counts,
):
    _, slots, edge, _, data = features.shape
    in_width, width = conv_first.shape[-2:]
    classes = head_bias.shape[1]
    peers = lax.axis_size("folds") * lax.axis_size("sub")
    tiles = lax.axis_size("tiles")
    chunk = VX // peers
    area = edge * edge
    lanes = edge * classes
    padded = slots * (area + edge) + edge
    middle = chunk * 2 // 5
    halves = ((0, middle), (middle, chunk))
    parts = [(0, 0, chunk, True)]
    for low_row, high_row in halves:
        parts += [
            (peer, low_row, high_row, peer == 1 and low_row > 0)
            for peer in [*range(2, peers), 1]
        ]
    rows = [
        slots * edge * (high_row - low_row) + (edge if noted else 0)
        for _, low_row, high_row, noted in parts
    ]
    pieces = pl.pallas_call(
        functools.partial(section_kernel, (slots, edge, chunk, parts)),
        out_shape=[pltpu.VMEM((count, lanes), bf16) for count in rows],
        in_specs=[hbm] * 11,
        out_specs=[vmem] * len(parts),
        scratch_shapes=[
            pltpu.VMEM((padded, data + 256), bf16),
            pltpu.VMEM((padded, edge * width + 128), bf16),
            pltpu.VMEM((padded, edge * width), bf16),
            pltpu.VMEM((2, 768, 256), bf16),
            pltpu.VMEM((2, 384, 256), bf16),
            pltpu.VMEM((padded - 2 * edge, edge * width + 128), f32),
            pltpu.VMEM((padded - 2 * edge, edge * width), f32),
            pltpu.SMEM(corners.shape, jnp.int32),
            pltpu.SMEM(counts.shape[::-1], jnp.int32),
            pltpu.VMEM((27 * width, in_width), bf16),
            pltpu.VMEM((1, width), f32),
            pltpu.VMEM((1, width), f32),
            pltpu.VMEM((27 * width, width), bf16),
            pltpu.VMEM((1, width), f32),
            pltpu.VMEM((1, width), f32),
            pltpu.VMEM((classes, width), bf16),
            pltpu.VMEM((1, classes), f32),
            pltpu.VMEM((slots, VX * edge, area), bf16),
            pltpu.SemaphoreType.DMA((10 + slots,)),
        ],
        compiler_params=ample,
        name="section",
    )(
        corners,
        counts.T,
        features.reshape(slots, area, data),
        jnp.swapaxes(conv_first, 4, 5).reshape(27 * width, in_width),
        gain_first,
        shift_first,
        conv_second.reshape(27 * width, width),
        gain_second,
        shift_second,
        head_weight[0].T,
        head_bias,
    )
    arrived = []
    for (peer, _, _, _), piece in zip(parts, pieces):
        pairs = [(i, i ^ peer) for i in range(peers)]
        arrived.append(lax.ppermute(piece, ("folds", "sub"), pairs) if peer else piece)

    def gather(first, last, spilled, kind, name):
        chosen = [
            (part, piece)
            for part, piece in zip(parts, arrived)
            if part[3] or (part[1] < last and first < part[2])
        ]
        return pl.pallas_call(
            functools.partial(
                gather_kernel,
                (slots, edge, chunk, [part for part, _ in chosen], first, last, classes),
                spilled,
            ),
            out_shape=pltpu.VMEM((last - first, TZ, VY * classes), kind),
            in_specs=[vmem] * len(chosen),
            out_specs=vmem,
            compiler_params=limits,
            cost_estimate=pl.CostEstimate(
                flops=500000000, bytes_accessed=2000000, transcendentals=0
            ),
            name=name,
        )(*[piece for _, piece in chosen])

    even = [(tile, tile ^ 1) for tile in range(tiles)]
    odd = []
    for tile in range(tiles):
        for i in range(peers):
            if 0 < tile < tiles - 1:
                target = (tile + 1 if tile % 2 else tile - 1) * peers + i
            else:
                target = tile * peers + (i ^ 1)
            odd.append((tile * peers + i, target))
    from_below = []
    for first, last in halves:
        spill = gather(first, last, True, bf16, f"spill_{first}")
        from_below.append(lax.ppermute(spill, ("tiles", "folds", "sub"), odd))
        from_below.append(lax.ppermute(spill, "tiles", even))
    own = gather(0, chunk, False, f32, "own")
    joined = None
    for at in (1, 0):
        low_row, high_row = halves[at]
        joined = pl.pallas_call(
            functools.partial(join_kernel, low_row),
            out_shape=jax.ShapeDtypeStruct((chunk, TZ, VY * classes), f32),
            in_specs=[vmem] * 3 + ([] if joined is None else [hbm]),
            out_specs=hbm,
            input_output_aliases={} if joined is None else {3: 0},
            scratch_shapes=[
                pltpu.VMEM((high_row - low_row, TZ, VY * classes), f32),
                pltpu.SemaphoreType.DMA((high_row - low_row,)),
            ],
            compiler_params=limits,
            name=f"join_{low_row}",
        )(own, *from_below[2 * at : 2 * at + 2], *([] if joined is None else [joined]))
    return jnp.transpose(joined, (1, 0, 2))


def solution(mesh):
    placed = (
        P("folds", ("groups", "tiles", "sub"), None, None, None),
        P("folds", None, None, None, None, None),
        P("folds", None),
        P("folds", None),
        P("folds", None, None, None, None, None),
        P("folds", None),
        P("folds", None),
        P("folds", None, None),
        P("folds", None),
        P(("groups", "tiles", "sub"), None),
        P("groups", None),
    )
    return jax.shard_map(
        on_device,
        mesh=mesh,
        in_specs=placed,
        out_specs=P(("groups", "tiles"), ("folds", "sub"), None),
        check_vma=False,
    )
```

profile of v0, /device:TPU:0, one launch (start us, length us, event | category | flops | bytes accessed | tf_op | source)
XLA Modules:
  0.0 23.9 jit_solution(4000297246381490262)
XLA Ops:
  0.0 7.3 %section.1 = (bf16[336,256]{1,0:T(8,128)(2,1)S(1)}, bf16[128,256]{1,0:T(8,128)(2,1)S(1)}, bf16[128,256]{1,0:T(8,128)(2,1)S(1)}, bf16[128,256]{1,0:T(8,128)(2,1)S...) custom-call(s32[2,3]{1,0:T(2,128)} %corners_hbm.1, ...), custom_call_target="tpu_custom_call" | custom-call | tf_op jit(solution)/shard_map/section/pallas_call | solution.py:475
  7.3 3.0 %collective-permute-start.3 = (bf16[192,256]{1,0:T(8,128)(2,1)S(1)}, bf16[192,256]{1,0:T(8,128)(2,1)S(1)}, u32[]{:S(2)}, u32[]{:S(2)}) collective-permute-start(bf16[192,256]{1,0:T(8,128)(2,1)S(1)} %get-tuple-element.16), channel_id=1, source_target_pairs={{0,2},{1,3},{2,0},{3,1},{4,6},{5,7},{6,4},{7,5},{8,10},{9,11},{10,... | collective-permute-start | bytes 294920 | tf_op jit(solution)/shard_map/ppermute | solution.py:519
  10.3 0.0 collective-permute-start.5
  10.3 0.2 collective-permute-start.4
  10.5 1.9 %collective-permute-start = (bf16[128,256]{1,0:T(8,128)(2,1)S(1)}, bf16[128,256]{1,0:T(8,128)(2,1)S(1)}, u32[]{:S(2)}, u32[]{:S(2)}) collective-permute-start(bf16[128,256]{1,0:T(8,128)(2,1)S(1)} %get-tuple-element.13), channel_id=1, source_target_pairs={{0,2},{1,3},{2,0},{3,1},{4,6},{5,7},{6,4},{7,5},{8,10},{9,11},{10,... | collective-permute-start | bytes 196616 | tf_op jit(solution)/shard_map/ppermute | solution.py:519
  12.5 0.0 collective-permute-start.1
  12.5 1.1 %collective-permute-done.3.rest_4_.rest_1_ = bf16[192,256]{1,0:T(8,128)(2,1)S(1)} collective-permute-done((bf16[192,256]{1,0:T(8,128)(2,1)S(1)}, bf16[192,256]{1,0:T(8,128)(2,1)S(1)}, u32[]{:S(2)}, u32[]{:S(2)}) %collective-permute-start.3) | collective-permute-done | bytes 98336 | tf_op jit(solution)/shard_map/ppermute | solution.py:519
  13.5 0.0 collective-permute-start.2
  13.5 2.1 %collective-permute-done.4.rest_5_.rest_2_ = bf16[192,256]{1,0:T(8,128)(2,1)S(1)} collective-permute-done((bf16[192,256]{1,0:T(8,128)(2,1)S(1)}, bf16[192,256]{1,0:T(8,128)(2,1)S(1)}, u32[]{:S(2)}, u32[]{:S(2)}) %collective-permute-start.4) | collective-permute-done | bytes 98336 | tf_op jit(solution)/shard_map/ppermute | solution.py:519
  15.7 0.2 spill_4.1
  15.8 1.6 %collective-permute-start.9 = (bf16[6,16,640]{2,1,0:T(8,128)(2,1)S(1)}, bf16[6,16,640]{2,1,0:T(8,128)(2,1)S(1)}, u32[]{:S(2)}, u32[]{:S(2)}) collective-permute-start(bf16[6,16,640]{2,1,0:T(8,128)(2,1)S(1)} %spill_4.1), channel_id=1, source_target_pairs={{0,4},{4,0},{8,12},{12,8},{1,5},{5,1},{9,13},{13,9},{2,6},{6,2},{1... | collective-permute-start | bytes 368648 | tf_op jit(solution)/shard_map/ppermute | solution.py:556
  17.4 0.0 collective-permute-start.8
  17.4 0.0 collective-permute-done.rest_1_
  17.5 0.1 collective-permute-done.1.rest_2_
  17.6 0.0 collective-permute-done.2.rest_3_
  17.6 0.1 spill_0.1
  17.7 3.1 %collective-permute-start.7 = (bf16[4,16,640]{2,1,0:T(8,128)(2,1)S(1)}, bf16[4,16,640]{2,1,0:T(8,128)(2,1)S(1)}, u32[]{:S(2)}, u32[]{:S(2)}) collective-permute-start(bf16[4,16,640]{2,1,0:T(8,128)(2,1)S(1)} %spill_0.1), channel_id=1, source_target_pairs={{0,4},{4,0},{8,12},{12,8},{1,5},{5,1},{9,13},{13,9},{2,6},{6,2},{1... | collective-permute-start | bytes 245768 | tf_op jit(solution)/shard_map/ppermute | solution.py:556
  20.8 0.0 collective-permute-start.6
  20.8 0.2 own.1.own_ref
  21.1 0.3 %collective-permute-done.9.even_ref = bf16[6,16,640]{2,1,0:T(8,128)(2,1)S(1)} collective-permute-done((bf16[6,16,640]{2,1,0:T(8,128)(2,1)S(1)}, bf16[6,16,640]{2,1,0:T(8,128)(2,1)S(1)}, u32[]{:S(2)}, u32[]{:S(2)}) %collective-permute-start.9) | collective-permute-done | bytes 122912 | tf_op jit(solution)/shard_map/ppermute | solution.py:556
  21.4 0.8 %join_4.1.rest_0_ = f32[10,16,640]{2,1,0:T(8,128)} custom-call(f32[10,16,640]{2,1,0:T(8,128)S(1)} %own.1.own_ref, bf16[6,16,640]{2,1,0:T(8,128)(2,1)S(1)} %collective-permute-done.8.odd_ref, bf16[6,16,640]{2,1,0:T(8,128)(2,1)S(1)} %collective-permute-done.9.even_ref), custom_call_target="tpu_custom_call" | custom-call | tf_op jit(solution)/shard_map/join_4/pallas_call | solution.py:561
  22.1 1.1 %collective-permute-done.7.even_ref = bf16[4,16,640]{2,1,0:T(8,128)(2,1)S(1)} collective-permute-done((bf16[4,16,640]{2,1,0:T(8,128)(2,1)S(1)}, bf16[4,16,640]{2,1,0:T(8,128)(2,1)S(1)}, u32[]{:S(2)}, u32[]{:S(2)}) %collective-permute-start.7) | collective-permute-done | bytes 81952 | tf_op jit(solution)/shard_map/ppermute | solution.py:556
  23.2 0.0 collective-permute-done.6.odd_ref
  23.2 0.7 %join_0.1 = f32[10,16,640]{2,1,0:T(8,128)} custom-call(f32[10,16,640]{2,1,0:T(8,128)S(1)} %own.1.own_ref, bf16[4,16,640]{2,1,0:T(8,128)(2,1)S(1)} %collective-permute-done.6.odd_ref, bf16[4,16,640]{2,1,0:T(8,128)(2,1)S(1)} %collective-permute-done.7.even_ref, f32[10,16,640]{2,1,0:T(8,128)} %join_4.1.rest_0_), custom_call_target="tpu_custom_call", output_to_operand_aliasing={{}: (3, {})} | custom-call | tf_op jit(solution)/shard_map/join_0/pallas_call | solution.py:561
  (2 shorter events, 0.0 us)
Async XLA Ops:
  7.3 6.2 %collective-permute-start.3 = (bf16[192,256]{1,0:T(8,128)(2,1)S(1)}, bf16[192,256]{1,0:T(8,128)(2,1)S(1)}, u32[]{:S(2)}, u32[]{:S(2)}) collective-permute-start(bf16[192,256]{1,0:T(8,128)(2,1)S(1)} %get-tuple-element.16), channel_id=1, source_target_pairs={{0,2},{1,3},{2,0},{3,1},{4,6},{5,7},{6,4},{7,5},{8,10},{9,11},{10,... | collective-permute-start | bytes 294920 | tf_op jit(solution)/shard_map/ppermute | solution.py:519
  10.3 5.3 %collective-permute-start.5 = (bf16[208,256]{1,0:T(8,128)(2,1)S(1)}, bf16[208,256]{1,0:T(8,128)(2,1)S(1)}, u32[]{:S(2)}, u32[]{:S(2)}) collective-permute-start(bf16[208,256]{1,0:T(8,128)(2,1)S(1)} %get-tuple-element.18), channel_id=1, source_target_pairs={{0,1},{1,0},{2,3},{3,2},{4,5},{5,4},{6,7},{7,6},{8,9},{9,8},{10,11... | collective-permute-start | bytes 319496 | tf_op jit(solution)/shard_map/ppermute | solution.py:519
  10.3 5.3 %collective-permute-start.4 = (bf16[192,256]{1,0:T(8,128)(2,1)S(1)}, bf16[192,256]{1,0:T(8,128)(2,1)S(1)}, u32[]{:S(2)}, u32[]{:S(2)}) collective-permute-start(bf16[192,256]{1,0:T(8,128)(2,1)S(1)} %get-tuple-element.17), channel_id=1, source_target_pairs={{0,3},{1,2},{2,1},{3,0},{4,7},{5,6},{6,5},{7,4},{8,11},{9,10},{10,... | collective-permute-start | bytes 294920 | tf_op jit(solution)/shard_map/ppermute | solution.py:519
  10.5 6.9 %collective-permute-start = (bf16[128,256]{1,0:T(8,128)(2,1)S(1)}, bf16[128,256]{1,0:T(8,128)(2,1)S(1)}, u32[]{:S(2)}, u32[]{:S(2)}) collective-permute-start(bf16[128,256]{1,0:T(8,128)(2,1)S(1)} %get-tuple-element.13), channel_id=1, source_target_pairs={{0,2},{1,3},{2,0},{3,1},{4,6},{5,7},{6,4},{7,5},{8,10},{9,11},{10,... | collective-permute-start | bytes 196616 | tf_op jit(solution)/shard_map/ppermute | solution.py:519
  12.5 5.1 %collective-permute-start.1 = (bf16[128,256]{1,0:T(8,128)(2,1)S(1)}, bf16[128,256]{1,0:T(8,128)(2,1)S(1)}, u32[]{:S(2)}, u32[]{:S(2)}) collective-permute-start(bf16[128,256]{1,0:T(8,128)(2,1)S(1)} %get-tuple-element.14), channel_id=1, source_target_pairs={{0,3},{1,2},{2,1},{3,0},{4,7},{5,6},{6,5},{7,4},{8,11},{9,10},{10,... | collective-permute-start | bytes 196616 | tf_op jit(solution)/shard_map/ppermute | solution.py:519
  13.5 4.1 %collective-permute-start.2 = (bf16[128,256]{1,0:T(8,128)(2,1)S(1)}, bf16[128,256]{1,0:T(8,128)(2,1)S(1)}, u32[]{:S(2)}, u32[]{:S(2)}) collective-permute-start(bf16[128,256]{1,0:T(8,128)(2,1)S(1)} %get-tuple-element.15), channel_id=1, source_target_pairs={{0,1},{1,0},{2,3},{3,2},{4,5},{5,4},{6,7},{7,6},{8,9},{9,8},{10,11... | collective-permute-start | bytes 196616 | tf_op jit(solution)/shard_map/ppermute | solution.py:519
  15.8 5.5 %collective-permute-start.9 = (bf16[6,16,640]{2,1,0:T(8,128)(2,1)S(1)}, bf16[6,16,640]{2,1,0:T(8,128)(2,1)S(1)}, u32[]{:S(2)}, u32[]{:S(2)}) collective-permute-start(bf16[6,16,640]{2,1,0:T(8,128)(2,1)S(1)} %spill_4.1), channel_id=1, source_target_pairs={{0,4},{4,0},{8,12},{12,8},{1,5},{5,1},{9,13},{13,9},{2,6},{6,2},{1... | collective-permute-start | bytes 368648 | tf_op jit(solution)/shard_map/ppermute | solution.py:556
  17.4 3.9 %collective-permute-start.8 = (bf16[6,16,640]{2,1,0:T(8,128)(2,1)S(1)}, bf16[6,16,640]{2,1,0:T(8,128)(2,1)S(1)}, u32[]{:S(2)}, u32[]{:S(2)}) collective-permute-start(bf16[6,16,640]{2,1,0:T(8,128)(2,1)S(1)} %spill_4.1), channel_id=1, source_target_pairs={{0,1},{1,0},{2,3},{3,2},{4,8},{5,9},{6,10},{7,11},{8,4},{9,5},{10,... | collective-permute-start | bytes 368648 | tf_op jit(solution)/shard_map/ppermute | solution.py:555
  17.7 5.5 %collective-permute-start.7 = (bf16[4,16,640]{2,1,0:T(8,128)(2,1)S(1)}, bf16[4,16,640]{2,1,0:T(8,128)(2,1)S(1)}, u32[]{:S(2)}, u32[]{:S(2)}) collective-permute-start(bf16[4,16,640]{2,1,0:T(8,128)(2,1)S(1)} %spill_0.1), channel_id=1, source_target_pairs={{0,4},{4,0},{8,12},{12,8},{1,5},{5,1},{9,13},{13,9},{2,6},{6,2},{1... | collective-permute-start | bytes 245768 | tf_op jit(solution)/shard_map/ppermute | solution.py:556
  20.8 2.4 %collective-permute-start.6 = (bf16[4,16,640]{2,1,0:T(8,128)(2,1)S(1)}, bf16[4,16,640]{2,1,0:T(8,128)(2,1)S(1)}, u32[]{:S(2)}, u32[]{:S(2)}) collective-permute-start(bf16[4,16,640]{2,1,0:T(8,128)(2,1)S(1)} %spill_0.1), channel_id=1, source_target_pairs={{0,1},{1,0},{2,3},{3,2},{4,8},{5,9},{6,10},{7,11},{8,4},{9,5},{10,... | collective-permute-start | bytes 245768 | tf_op jit(solution)/shard_map/ppermute | solution.py:555
where the time goes:
time: 24.1 us; the launch traced here: 23.9 us
  starting transfers between devices  9.85 us (41%)
  Pallas kernels  9.32 us (39%)
  waiting for transfers between devices  4.73 us (20%)
    pallas_call x1, Pallas kernels, on_device(): pl.pallas_call(functools.partial(section_kernel, (slots, edge, chunk, par...  7.32 us
    ppermute x6, starting transfers between devices, on_device(): lax.ppermute(piece, ('folds', 'sub'), pairs)  5.15 us
    ppermute x2, starting transfers between devices, on_device(): from_below.append(lax.ppermute(spill, 'tiles', even))  4.7 us
    ppermute x6, waiting for transfers between devices, on_device(): lax.ppermute(piece, ('folds', 'sub'), pairs)  3.32 us
    pallas_call x2, Pallas kernels, on_device(): pl.pallas_call(functools.partial(join_kernel, low_row), out_shape=jax.Sha...  1.47 us
    ppermute x2, waiting for transfers between devices, on_device(): from_below.append(lax.ppermute(spill, 'tiles', even))  1.41 us
    pallas_call x3, Pallas kernels, gather(): pl.pallas_call(functools.partial(gather_kernel, (slots, edge, chunk, [par...  0.53 us
  transfers between devices with their start and end apart: 10, of which 5 were waited for; matrix products, arithmetic and copies ran while one was open for 0% of the time, Pallas kernels for 5%

commit v1 on v0

--- a/solution.py
+++ b/solution.py
@@ -53,6 +53,9 @@
                 empty = here if empty is None else empty | here
         total = jnp.where(empty, 0.0, total)
     return total
+
+
+OUTER = ({2: 0, 3: 1}, {0: 1, 1: 2})
 
 
 def build_pairs(taps_ref, band_ref, in_width, width, swapped, dz):
@@ -75,13 +78,14 @@
         wide = jnp.dot(taps_ref[at : at + 9 * in_width], spread, preferred_element_type=f32)
         for tap in range(9):
             tiled[divmod(tap, 3)] = wide[tap * in_width : (tap + 1) * in_width]
-    for variant in range(2):
+    for variant in range(band_ref.shape[0]):
         for yi in range(4):
             for side in range(2):
                 parts = []
-                for dx in orders[variant][side]:
+                for dx in orders[variant % 2][side]:
                     for yo in range(2):
-                        parts.append(None if dx is None else tiled.get((dx, yi - yo)))
+                        dy = OUTER[yo].get(yi) if variant == 2 else yi - yo
+                        parts.append(None if dx is None else tiled.get((dx, dy)))
                 block = lane_bands(parts, places)
                 at = (dz * 4 + yi) * in_width
                 band_ref[variant, at : at + in_width, side * 128 : (side + 1) * 128] = (
@@ -89,9 +93,13 @@
                 )
 
 
-def banded(pad_ref, lane, count, edge, band):
-    depth = band.shape[0] // 3
-    view = [pad_ref[dz * edge : dz * edge + count, lane : lane + depth] for dz in range(3)]
+def banded(pad_ref, starts, count, edge, band):
+    depth = band.shape[0] // (3 * len(starts))
+    view = [
+        pad_ref[dz * edge : dz * edge + count, lane : lane + depth]
+        for dz in range(3)
+        for lane in starts
+    ]
     return jnp.dot(jnp.concatenate(view, axis=1), band, preferred_element_type=f32)
 
 
@@ -228,9 +236,6 @@
     for pad in (pad_one, pad_two, pad_turned):
         for slot in range(slots + 1):
             pad[slot * stride : slot * stride + edge, :] = jnp.zeros((edge, pad.shape[1]), bf16)
-    pad_one[:, :128] = jnp.zeros((pad_one.shape[0], 128), bf16)
-    pad_one[:, 128 + data :] = jnp.zeros((pad_one.shape[0], 128), bf16)
-
     center, spread = (edge - 1) / 2.0, edge / 4.0
 
     def profile(offset):
@@ -291,11 +296,15 @@
     masks[0] = spot >= width
     masks[-1] = spot < width
     norms = [Norm(width, area, voxels) for _ in range(slots)]
+    outer = banded(pad_one, [128, data], count, edge, band_one[2])
     for pair in range(pairs):
-        even = banded(pad_one, 256 * pair, count, edge, band_one[0])
+        if 0 < pair < pairs - 1:
+            even = banded(pad_one, [256 * pair], count, edge, band_one[0])
+        else:
+            even = outer
         odd = None
         if pair < pairs - 1:
-            odd = banded(pad_one, 256 * pair + 128, count, edge, band_one[1])
+            odd = banded(pad_one, [256 * pair + 128], count, edge, band_one[1])
         block = join_pair(even, odd, low, across, edge)
         hidden[:, pair * 128 : (pair + 1) * 128] = block
         for slot, norm in enumerate(norms):
@@ -335,8 +344,8 @@
     refresh(0)
     for quad in range(quads):
         refresh(quad + 1)
-        even = banded(pad_two, 128 * quad, count, edge, band_two[0])
-        odd = banded(pad_turned, 128 * quad, count, edge, band_two[1])
+        even = banded(pad_two, [128 * quad], count, edge, band_two[0])
+        odd = banded(pad_turned, [128 * quad], count, edge, band_two[1])
         block = join_pair(even, odd, low, across, edge)
         outcome[:, quad * 128 : (quad + 1) * 128] = block
         for slot, norm in enumerate(seconds):
@@ -481,7 +490,7 @@
             pltpu.VMEM((padded, data + 256), bf16),
             pltpu.VMEM((padded, edge * width + 128), bf16),
             pltpu.VMEM((padded, edge * width), bf16),
-            pltpu.VMEM((2, 768, 256), bf16),
+            pltpu.VMEM((3, 768, 256), bf16),
             pltpu.VMEM((2, 384, 256), bf16),
             pltpu.VMEM((padded - 2 * edge, edge * width + 128), f32),
             pltpu.VMEM((padded - 2 * edge, edge * width), f32),

time: 24.1 us -> 23.5 us (0.975)
  Pallas kernels: 9.32 us -> 8.78 us
    pallas_call x1, Pallas kernels: 7.32 us -> 6.78 us  [on_device(): pl.pallas_call(functools.partial(section_kernel, (slots, edge, chunk, par...]
where the time goes in v1:
time: 23.5 us; the launch traced here: 23.4 us
  starting transfers between devices  9.87 us (42%)
  Pallas kernels  8.78 us (37%)
  waiting for transfers between devices  4.72 us (20%)
    pallas_call x1, Pallas kernels, on_device(): pl.pallas_call(functools.partial(section_kernel, (slots, edge, chunk, par...  6.78 us
    ppermute x6, starting transfers between devices, on_device(): lax.ppermute(piece, ('folds', 'sub'), pairs)  5.14 us
    ppermute x2, starting transfers between devices, on_device(): from_below.append(lax.ppermute(spill, 'tiles', even))  4.72 us
    ppermute x6, waiting for transfers between devices, on_device(): lax.ppermute(piece, ('folds', 'sub'), pairs)  3.31 us
    pallas_call x2, Pallas kernels, on_device(): pl.pallas_call(functools.partial(join_kernel, low_row), out_shape=jax.Sha...  1.47 us
    ppermute x2, waiting for transfers between devices, on_device(): from_below.append(lax.ppermute(spill, 'tiles', even))  1.41 us
    pallas_call x3, Pallas kernels, gather(): pl.pallas_call(functools.partial(gather_kernel, (slots, edge, chunk, [par...  0.53 us
  transfers between devices with their start and end apart: 10, of which 5 were waited for; matrix products, arithmetic and copies ran while one was open for 0% of the time, Pallas kernels for 5%

profile of v1, /device:TPU:0, one launch (start us, length us, event | category | flops | bytes accessed | tf_op | source)
XLA Modules:
  0.0 23.4 jit_solution(12178323090940049370)
XLA Ops:
  0.0 6.8 %section.1 = (bf16[336,256]{1,0:T(8,128)(2,1)S(1)}, bf16[128,256]{1,0:T(8,128)(2,1)S(1)}, bf16[128,256]{1,0:T(8,128)(2,1)S(1)}, bf16[128,256]{1,0:T(8,128)(2,1)S...) custom-call(s32[2,3]{1,0:T(2,128)} %corners_hbm.1, ...), custom_call_target="tpu_custom_call" | custom-call | tf_op jit(solution)/shard_map/section/pallas_call | solution.py:484
  6.8 3.0 %collective-permute-start.3 = (bf16[192,256]{1,0:T(8,128)(2,1)S(1)}, bf16[192,256]{1,0:T(8,128)(2,1)S(1)}, u32[]{:S(2)}, u32[]{:S(2)}) collective-permute-start(bf16[192,256]{1,0:T(8,128)(2,1)S(1)} %get-tuple-element.16), channel_id=1, source_target_pairs={{0,2},{1,3},{2,0},{3,1},{4,6},{5,7},{6,4},{7,5},{8,10},{9,11},{10,... | collective-permute-start | bytes 294920 | tf_op jit(solution)/shard_map/ppermute | solution.py:528
  9.8 0.0 collective-permute-start.5
  9.8 0.2 collective-permute-start.4
  10.0 1.9 %collective-permute-start = (bf16[128,256]{1,0:T(8,128)(2,1)S(1)}, bf16[128,256]{1,0:T(8,128)(2,1)S(1)}, u32[]{:S(2)}, u32[]{:S(2)}) collective-permute-start(bf16[128,256]{1,0:T(8,128)(2,1)S(1)} %get-tuple-element.13), channel_id=1, source_target_pairs={{0,2},{1,3},{2,0},{3,1},{4,6},{5,7},{6,4},{7,5},{8,10},{9,11},{10,... | collective-permute-start | bytes 196616 | tf_op jit(solution)/shard_map/ppermute | solution.py:528
  11.9 0.0 collective-permute-start.1
  11.9 1.1 %collective-permute-done.3.rest_4_.rest_1_ = bf16[192,256]{1,0:T(8,128)(2,1)S(1)} collective-permute-done((bf16[192,256]{1,0:T(8,128)(2,1)S(1)}, bf16[192,256]{1,0:T(8,128)(2,1)S(1)}, u32[]{:S(2)}, u32[]{:S(2)}) %collective-permute-start.3) | collective-permute-done | bytes 98336 | tf_op jit(solution)/shard_map/ppermute | solution.py:528
  13.0 2.1 %collective-permute-done.4.rest_5_.rest_2_ = bf16[192,256]{1,0:T(8,128)(2,1)S(1)} collective-permute-done((bf16[192,256]{1,0:T(8,128)(2,1)S(1)}, bf16[192,256]{1,0:T(8,128)(2,1)S(1)}, u32[]{:S(2)}, u32[]{:S(2)}) %collective-permute-start.4) | collective-permute-done | bytes 98336 | tf_op jit(solution)/shard_map/ppermute | solution.py:528
  15.1 0.2 spill_4.1
  15.3 1.6 %collective-permute-start.9 = (bf16[6,16,640]{2,1,0:T(8,128)(2,1)S(1)}, bf16[6,16,640]{2,1,0:T(8,128)(2,1)S(1)}, u32[]{:S(2)}, u32[]{:S(2)}) collective-permute-start(bf16[6,16,640]{2,1,0:T(8,128)(2,1)S(1)} %spill_4.1), channel_id=1, source_target_pairs={{0,4},{4,0},{8,12},{12,8},{1,5},{5,1},{9,13},{13,9},{2,6},{6,2},{1... | collective-permute-start | bytes 368648 | tf_op jit(solution)/shard_map/ppermute | solution.py:565
  16.9 0.0 collective-permute-start.8
  16.9 0.0 collective-permute-done.rest_1_
  16.9 0.1 collective-permute-done.1.rest_2_
  17.0 0.0 collective-permute-done.2.rest_3_
  17.1 0.1 spill_0.1
  17.2 3.1 %collective-permute-start.7 = (bf16[4,16,640]{2,1,0:T(8,128)(2,1)S(1)}, bf16[4,16,640]{2,1,0:T(8,128)(2,1)S(1)}, u32[]{:S(2)}, u32[]{:S(2)}) collective-permute-start(bf16[4,16,640]{2,1,0:T(8,128)(2,1)S(1)} %spill_0.1), channel_id=1, source_target_pairs={{0,4},{4,0},{8,12},{12,8},{1,5},{5,1},{9,13},{13,9},{2,6},{6,2},{1... | collective-permute-start | bytes 245768 | tf_op jit(solution)/shard_map/ppermute | solution.py:565
  20.3 0.0 collective-permute-start.6
  20.3 0.2 %own.1.own_ref = f32[10,16,640]{2,1,0:T(8,128)S(1)} custom-call(bf16[336,256]{1,0:T(8,128)(2,1)S(1)} %get-tuple-element.12.rest_0_, bf16[128,256]{1,0:T(8,128)(2,1)S(1)} %collective-permute-done.rest_1_, bf16[128,256]{1,0:T(8,128)(2,1)S(1)} %collective-permute-done.1.rest_2_, bf16[128,256]{1,0:T(8,128)(2,1)S(1)} %collective-permute-done.2.rest_3_, ...), custom_call_target="tpu_custom_call" | custom-call | flops 500000000 | bytes 2000000 | tf_op jit(solution)/shard_map/own/pallas_call | solution.py:536
  20.5 0.3 %collective-permute-done.9.even_ref = bf16[6,16,640]{2,1,0:T(8,128)(2,1)S(1)} collective-permute-done((bf16[6,16,640]{2,1,0:T(8,128)(2,1)S(1)}, bf16[6,16,640]{2,1,0:T(8,128)(2,1)S(1)}, u32[]{:S(2)}, u32[]{:S(2)}) %collective-permute-start.9) | collective-permute-done | bytes 122912 | tf_op jit(solution)/shard_map/ppermute | solution.py:565
  20.8 0.0 collective-permute-done.8.odd_ref
  20.8 0.8 %join_4.1.rest_0_ = f32[10,16,640]{2,1,0:T(8,128)} custom-call(f32[10,16,640]{2,1,0:T(8,128)S(1)} %own.1.own_ref, bf16[6,16,640]{2,1,0:T(8,128)(2,1)S(1)} %collective-permute-done.8.odd_ref, bf16[6,16,640]{2,1,0:T(8,128)(2,1)S(1)} %collective-permute-done.9.even_ref), custom_call_target="tpu_custom_call" | custom-call | tf_op jit(solution)/shard_map/join_4/pallas_call | solution.py:570
  21.6 1.1 %collective-permute-done.7.even_ref = bf16[4,16,640]{2,1,0:T(8,128)(2,1)S(1)} collective-permute-done((bf16[4,16,640]{2,1,0:T(8,128)(2,1)S(1)}, bf16[4,16,640]{2,1,0:T(8,128)(2,1)S(1)}, u32[]{:S(2)}, u32[]{:S(2)}) %collective-permute-start.7) | collective-permute-done | bytes 81952 | tf_op jit(solution)/shard_map/ppermute | solution.py:565
  22.7 0.0 collective-permute-done.6.odd_ref
  22.7 0.7 %join_0.1 = f32[10,16,640]{2,1,0:T(8,128)} custom-call(f32[10,16,640]{2,1,0:T(8,128)S(1)} %own.1.own_ref, bf16[4,16,640]{2,1,0:T(8,128)(2,1)S(1)} %collective-permute-done.6.odd_ref, bf16[4,16,640]{2,1,0:T(8,128)(2,1)S(1)} %collective-permute-done.7.even_ref, f32[10,16,640]{2,1,0:T(8,128)} %join_4.1.rest_0_), custom_call_target="tpu_custom_call", output_to_operand_aliasing={{}: (3, {})} | custom-call | tf_op jit(solution)/shard_map/join_0/pallas_call | solution.py:570
  (2 shorter events, 0.0 us)
Async XLA Ops:
  6.8 6.2 %collective-permute-start.3 = (bf16[192,256]{1,0:T(8,128)(2,1)S(1)}, bf16[192,256]{1,0:T(8,128)(2,1)S(1)}, u32[]{:S(2)}, u32[]{:S(2)}) collective-permute-start(bf16[192,256]{1,0:T(8,128)(2,1)S(1)} %get-tuple-element.16), channel_id=1, source_target_pairs={{0,2},{1,3},{2,0},{3,1},{4,6},{5,7},{6,4},{7,5},{8,10},{9,11},{10,... | collective-permute-start | bytes 294920 | tf_op jit(solution)/shard_map/ppermute | solution.py:528
  9.8 5.3 %collective-permute-start.5 = (bf16[208,256]{1,0:T(8,128)(2,1)S(1)}, bf16[208,256]{1,0:T(8,128)(2,1)S(1)}, u32[]{:S(2)}, u32[]{:S(2)}) collective-permute-start(bf16[208,256]{1,0:T(8,128)(2,1)S(1)} %get-tuple-element.18), channel_id=1, source_target_pairs={{0,1},{1,0},{2,3},{3,2},{4,5},{5,4},{6,7},{7,6},{8,9},{9,8},{10,11... | collective-permute-start | bytes 319496 | tf_op jit(solution)/shard_map/ppermute | solution.py:528
  9.8 5.3 %collective-permute-start.4 = (bf16[192,256]{1,0:T(8,128)(2,1)S(1)}, bf16[192,256]{1,0:T(8,128)(2,1)S(1)}, u32[]{:S(2)}, u32[]{:S(2)}) collective-permute-start(bf16[192,256]{1,0:T(8,128)(2,1)S(1)} %get-tuple-element.17), channel_id=1, source_target_pairs={{0,3},{1,2},{2,1},{3,0},{4,7},{5,6},{6,5},{7,4},{8,11},{9,10},{10,... | collective-permute-start | bytes 294920 | tf_op jit(solution)/shard_map/ppermute | solution.py:528
  10.0 6.9 %collective-permute-start = (bf16[128,256]{1,0:T(8,128)(2,1)S(1)}, bf16[128,256]{1,0:T(8,128)(2,1)S(1)}, u32[]{:S(2)}, u32[]{:S(2)}) collective-permute-start(bf16[128,256]{1,0:T(8,128)(2,1)S(1)} %get-tuple-element.13), channel_id=1, source_target_pairs={{0,2},{1,3},{2,0},{3,1},{4,6},{5,7},{6,4},{7,5},{8,10},{9,11},{10,... | collective-permute-start | bytes 196616 | tf_op jit(solution)/shard_map/ppermute | solution.py:528
  11.9 5.1 %collective-permute-start.1 = (bf16[128,256]{1,0:T(8,128)(2,1)S(1)}, bf16[128,256]{1,0:T(8,128)(2,1)S(1)}, u32[]{:S(2)}, u32[]{:S(2)}) collective-permute-start(bf16[128,256]{1,0:T(8,128)(2,1)S(1)} %get-tuple-element.14), channel_id=1, source_target_pairs={{0,3},{1,2},{2,1},{3,0},{4,7},{5,6},{6,5},{7,4},{8,11},{9,10},{10,... | collective-permute-start | bytes 196616 | tf_op jit(solution)/shard_map/ppermute | solution.py:528
  13.0 4.1 %collective-permute-start.2 = (bf16[128,256]{1,0:T(8,128)(2,1)S(1)}, bf16[128,256]{1,0:T(8,128)(2,1)S(1)}, u32[]{:S(2)}, u32[]{:S(2)}) collective-permute-start(bf16[128,256]{1,0:T(8,128)(2,1)S(1)} %get-tuple-element.15), channel_id=1, source_target_pairs={{0,1},{1,0},{2,3},{3,2},{4,5},{5,4},{6,7},{7,6},{8,9},{9,8},{10,11... | collective-permute-start | bytes 196616 | tf_op jit(solution)/shard_map/ppermute | solution.py:528
  15.3 5.5 %collective-permute-start.9 = (bf16[6,16,640]{2,1,0:T(8,128)(2,1)S(1)}, bf16[6,16,640]{2,1,0:T(8,128)(2,1)S(1)}, u32[]{:S(2)}, u32[]{:S(2)}) collective-permute-start(bf16[6,16,640]{2,1,0:T(8,128)(2,1)S(1)} %spill_4.1), channel_id=1, source_target_pairs={{0,4},{4,0},{8,12},{12,8},{1,5},{5,1},{9,13},{13,9},{2,6},{6,2},{1... | collective-permute-start | bytes 368648 | tf_op jit(solution)/shard_map/ppermute | solution.py:565
  16.9 3.9 %collective-permute-start.8 = (bf16[6,16,640]{2,1,0:T(8,128)(2,1)S(1)}, bf16[6,16,640]{2,1,0:T(8,128)(2,1)S(1)}, u32[]{:S(2)}, u32[]{:S(2)}) collective-permute-start(bf16[6,16,640]{2,1,0:T(8,128)(2,1)S(1)} %spill_4.1), channel_id=1, source_target_pairs={{0,1},{1,0},{2,3},{3,2},{4,8},{5,9},{6,10},{7,11},{8,4},{9,5},{10,... | collective-permute-start | bytes 368648 | tf_op jit(solution)/shard_map/ppermute | solution.py:564
  17.2 5.5 %collective-permute-start.7 = (bf16[4,16,640]{2,1,0:T(8,128)(2,1)S(1)}, bf16[4,16,640]{2,1,0:T(8,128)(2,1)S(1)}, u32[]{:S(2)}, u32[]{:S(2)}) collective-permute-start(bf16[4,16,640]{2,1,0:T(8,128)(2,1)S(1)} %spill_0.1), channel_id=1, source_target_pairs={{0,4},{4,0},{8,12},{12,8},{1,5},{5,1},{9,13},{13,9},{2,6},{6,2},{1... | collective-permute-start | bytes 245768 | tf_op jit(solution)/shard_map/ppermute | solution.py:565
  20.3 2.4 %collective-permute-start.6 = (bf16[4,16,640]{2,1,0:T(8,128)(2,1)S(1)}, bf16[4,16,640]{2,1,0:T(8,128)(2,1)S(1)}, u32[]{:S(2)}, u32[]{:S(2)}) collective-permute-start(bf16[4,16,640]{2,1,0:T(8,128)(2,1)S(1)} %spill_0.1), channel_id=1, source_target_pairs={{0,1},{1,0},{2,3},{3,2},{4,8},{5,9},{6,10},{7,11},{8,4},{9,5},{10,... | collective-permute-start | bytes 245768 | tf_op jit(solution)/shard_map/ppermute | solution.py:564

commit v2 on v1

--- a/solution.py
+++ b/solution.py
@@ -255,10 +255,11 @@
     sub_index = lax.axis_index("sub")
     position = lax.axis_index("folds") * lax.axis_size("sub") + sub_index
 
-    for copy in copies[:-slots]:
-        copy.wait()
+    copies[0].wait()
     for dz in range(3):
         build_pairs(taps_one_ref, band_one, in_width, width, True, dz)
+    for copy in copies[1:-slots]:
+        copy.wait()
     gain_one, shift_one = tiled_row(gain_one_ref, 128), tiled_row(shift_one_ref, 128)
     gain_two, shift_two = tiled_row(gain_two_ref, 128), tiled_row(shift_two_ref, 128)
 
@@ -357,29 +358,33 @@
     for norm in seconds:
         norm.settle(gain_two, shift_two)
 
+    normed = []
     for slot, norm in enumerate(seconds):
         at = slot * stride
-        logits = []
         for side in range(2):
-            normed = [
+            blocks = [
                 norm.give(outcome[at : at + area, quad * 128 : (quad + 1) * 128], None).astype(
                     bf16
                 )
                 for quad in range(side * quads // 2, (side + 1) * quads // 2)
             ]
-            logits.append(
-                jnp.dot(
-                    jnp.concatenate(normed, axis=1), head_block, preferred_element_type=f32
-                )
-            )
-        weighted = (jnp.concatenate(logits, axis=1) + bias) * gauss
+            normed.append(jnp.concatenate(blocks, axis=1))
+    logits = [jnp.dot(block, head_block, preferred_element_type=f32) for block in normed]
+    weighted = []
+    for slot in range(slots):
+        value = jnp.concatenate(logits[2 * slot : 2 * slot + 2], axis=1)
+        value = (value + bias) * gauss
         lane_start = corners_ref[slot, 2] * classes
-        weighted = pltpu.roll(weighted, lane_start % lanes, 1).astype(bf16)
-        placed = jnp.dot(selects[slot], weighted, preferred_element_type=f32).astype(bf16)
+        weighted.append(pltpu.roll(value, lane_start % lanes, 1).astype(bf16))
+    placed = [
+        jnp.dot(selects[slot], weighted[slot], preferred_element_type=f32).astype(bf16)
+        for slot in range(slots)
+    ]
+    for slot in range(slots):
         start = 0
         for (_, low_row, high_row, _), out_ref in zip(parts, out_refs):
             size = (high_row - low_row) * edge
-            out_ref[slot * size : (slot + 1) * size, :] = placed[start : start + size]
+            out_ref[slot * size : (slot + 1) * size, :] = placed[slot][start : start + size]
             start += size
 
 

time: 23.5 us -> 23.4 us (level)
  transfers between devices with their start and end apart: 10 -> 10, of which waited for: 5 -> 5; matrix products, arithmetic and copies ran while one was open for 0% -> 0% of each run, Pallas kernels for 5% -> 6%
where the time goes in v2:
time: 23.4 us; the launch traced here: 23.2 us
  starting transfers between devices  9.86 us (42%)
  Pallas kernels  8.58 us (37%)
  waiting for transfers between devices  4.73 us (20%)
    pallas_call x1, Pallas kernels, on_device(): pl.pallas_call(functools.partial(section_kernel, (slots, edge, chunk, par...  6.58 us
    ppermute x6, starting transfers between devices, on_device(): lax.ppermute(piece, ('folds', 'sub'), pairs)  5.16 us
    ppermute x2, starting transfers between devices, on_device(): from_below.append(lax.ppermute(spill, 'tiles', even))  4.7 us
    ppermute x6, waiting for transfers between devices, on_device(): lax.ppermute(piece, ('folds', 'sub'), pairs)  3.32 us
    pallas_call x2, Pallas kernels, on_device(): pl.pallas_call(functools.partial(join_kernel, low_row), out_shape=jax.Sha...  1.47 us
    ppermute x2, waiting for transfers between devices, on_device(): from_below.append(lax.ppermute(spill, 'tiles', even))  1.41 us
    pallas_call x3, Pallas kernels, gather(): pl.pallas_call(functools.partial(gather_kernel, (slots, edge, chunk, [par...  0.53 us
  transfers between devices with their start and end apart: 10, of which 5 were waited for; matrix products, arithmetic and copies ran while one was open for 0% of the time, Pallas kernels for 6%

profile of v2, /device:TPU:0, one launch (start us, length us, event | category | flops | bytes accessed | tf_op | source)
XLA Modules:
  0.0 23.2 jit_solution(16449158132327466432)
XLA Ops:
  0.0 6.6 %section.1 = (bf16[336,256]{1,0:T(8,128)(2,1)S(1)}, bf16[128,256]{1,0:T(8,128)(2,1)S(1)}, bf16[128,256]{1,0:T(8,128)(2,1)S(1)}, bf16[128,256]{1,0:T(8,128)(2,1)S...) custom-call(s32[2,3]{1,0:T(2,128)} %corners_hbm.1, ...), custom_call_target="tpu_custom_call" | custom-call | tf_op jit(solution)/shard_map/section/pallas_call | solution.py:489
  6.6 3.0 %collective-permute-start.3 = (bf16[192,256]{1,0:T(8,128)(2,1)S(1)}, bf16[192,256]{1,0:T(8,128)(2,1)S(1)}, u32[]{:S(2)}, u32[]{:S(2)}) collective-permute-start(bf16[192,256]{1,0:T(8,128)(2,1)S(1)} %get-tuple-element.16), channel_id=1, source_target_pairs={{0,2},{1,3},{2,0},{3,1},{4,6},{5,7},{6,4},{7,5},{8,10},{9,11},{10,... | collective-permute-start | bytes 294920 | tf_op jit(solution)/shard_map/ppermute | solution.py:533
  9.6 0.0 collective-permute-start.5
  9.6 0.2 collective-permute-start.4
  9.8 1.9 %collective-permute-start = (bf16[128,256]{1,0:T(8,128)(2,1)S(1)}, bf16[128,256]{1,0:T(8,128)(2,1)S(1)}, u32[]{:S(2)}, u32[]{:S(2)}) collective-permute-start(bf16[128,256]{1,0:T(8,128)(2,1)S(1)} %get-tuple-element.13), channel_id=1, source_target_pairs={{0,2},{1,3},{2,0},{3,1},{4,6},{5,7},{6,4},{7,5},{8,10},{9,11},{10,... | collective-permute-start | bytes 196616 | tf_op jit(solution)/shard_map/ppermute | solution.py:533
  11.7 0.0 collective-permute-start.1
  11.7 1.1 %collective-permute-done.3.rest_4_.rest_1_ = bf16[192,256]{1,0:T(8,128)(2,1)S(1)} collective-permute-done((bf16[192,256]{1,0:T(8,128)(2,1)S(1)}, bf16[192,256]{1,0:T(8,128)(2,1)S(1)}, u32[]{:S(2)}, u32[]{:S(2)}) %collective-permute-start.3) | collective-permute-done | bytes 98336 | tf_op jit(solution)/shard_map/ppermute | solution.py:533
  12.8 0.0 collective-permute-start.2
  12.8 2.1 %collective-permute-done.4.rest_5_.rest_2_ = bf16[192,256]{1,0:T(8,128)(2,1)S(1)} collective-permute-done((bf16[192,256]{1,0:T(8,128)(2,1)S(1)}, bf16[192,256]{1,0:T(8,128)(2,1)S(1)}, u32[]{:S(2)}, u32[]{:S(2)}) %collective-permute-start.4) | collective-permute-done | bytes 98336 | tf_op jit(solution)/shard_map/ppermute | solution.py:533
  14.9 0.0 collective-permute-done.5.rest_6_.rest_4_.rest_3_
  14.9 0.2 spill_4.1
  15.1 1.6 %collective-permute-start.9 = (bf16[6,16,640]{2,1,0:T(8,128)(2,1)S(1)}, bf16[6,16,640]{2,1,0:T(8,128)(2,1)S(1)}, u32[]{:S(2)}, u32[]{:S(2)}) collective-permute-start(bf16[6,16,640]{2,1,0:T(8,128)(2,1)S(1)} %spill_4.1), channel_id=1, source_target_pairs={{0,4},{4,0},{8,12},{12,8},{1,5},{5,1},{9,13},{13,9},{2,6},{6,2},{1... | collective-permute-start | bytes 368648 | tf_op jit(solution)/shard_map/ppermute | solution.py:570
  16.7 0.0 collective-permute-done.rest_1_
  16.7 0.1 collective-permute-done.1.rest_2_
  16.9 0.0 collective-permute-done.2.rest_3_
  16.9 0.1 spill_0.1
  17.0 3.1 %collective-permute-start.7 = (bf16[4,16,640]{2,1,0:T(8,128)(2,1)S(1)}, bf16[4,16,640]{2,1,0:T(8,128)(2,1)S(1)}, u32[]{:S(2)}, u32[]{:S(2)}) collective-permute-start(bf16[4,16,640]{2,1,0:T(8,128)(2,1)S(1)} %spill_0.1), channel_id=1, source_target_pairs={{0,4},{4,0},{8,12},{12,8},{1,5},{5,1},{9,13},{13,9},{2,6},{6,2},{1... | collective-permute-start | bytes 245768 | tf_op jit(solution)/shard_map/ppermute | solution.py:570
  20.1 0.2 %own.1.own_ref = f32[10,16,640]{2,1,0:T(8,128)S(1)} custom-call(bf16[336,256]{1,0:T(8,128)(2,1)S(1)} %get-tuple-element.12.rest_0_, bf16[128,256]{1,0:T(8,128)(2,1)S(1)} %collective-permute-done.rest_1_, bf16[128,256]{1,0:T(8,128)(2,1)S(1)} %collective-permute-done.1.rest_2_, bf16[128,256]{1,0:T(8,128)(2,1)S(1)} %collective-permute-done.2.rest_3_, ...), custom_call_target="tpu_custom_call" | custom-call | flops 500000000 | bytes 2000000 | tf_op jit(solution)/shard_map/own/pallas_call | solution.py:541
  20.3 0.3 %collective-permute-done.9.even_ref = bf16[6,16,640]{2,1,0:T(8,128)(2,1)S(1)} collective-permute-done((bf16[6,16,640]{2,1,0:T(8,128)(2,1)S(1)}, bf16[6,16,640]{2,1,0:T(8,128)(2,1)S(1)}, u32[]{:S(2)}, u32[]{:S(2)}) %collective-permute-start.9) | collective-permute-done | bytes 122912 | tf_op jit(solution)/shard_map/ppermute | solution.py:570
  20.6 0.0 collective-permute-done.8.odd_ref
  20.6 0.8 %join_4.1.rest_0_ = f32[10,16,640]{2,1,0:T(8,128)} custom-call(f32[10,16,640]{2,1,0:T(8,128)S(1)} %own.1.own_ref, bf16[6,16,640]{2,1,0:T(8,128)(2,1)S(1)} %collective-permute-done.8.odd_ref, bf16[6,16,640]{2,1,0:T(8,128)(2,1)S(1)} %collective-permute-done.9.even_ref), custom_call_target="tpu_custom_call" | custom-call | tf_op jit(solution)/shard_map/join_4/pallas_call | solution.py:575
  21.4 1.1 %collective-permute-done.7.even_ref = bf16[4,16,640]{2,1,0:T(8,128)(2,1)S(1)} collective-permute-done((bf16[4,16,640]{2,1,0:T(8,128)(2,1)S(1)}, bf16[4,16,640]{2,1,0:T(8,128)(2,1)S(1)}, u32[]{:S(2)}, u32[]{:S(2)}) %collective-permute-start.7) | collective-permute-done | bytes 81952 | tf_op jit(solution)/shard_map/ppermute | solution.py:570
  22.5 0.0 collective-permute-done.6.odd_ref
  22.5 0.7 %join_0.1 = f32[10,16,640]{2,1,0:T(8,128)} custom-call(f32[10,16,640]{2,1,0:T(8,128)S(1)} %own.1.own_ref, bf16[4,16,640]{2,1,0:T(8,128)(2,1)S(1)} %collective-permute-done.6.odd_ref, bf16[4,16,640]{2,1,0:T(8,128)(2,1)S(1)} %collective-permute-done.7.even_ref, f32[10,16,640]{2,1,0:T(8,128)} %join_4.1.rest_0_), custom_call_target="tpu_custom_call", output_to_operand_aliasing={{}: (3, {})} | custom-call | tf_op jit(solution)/shard_map/join_0/pallas_call | solution.py:575
  (2 shorter events, 0.0 us)
Async XLA Ops:
  6.6 6.2 %collective-permute-start.3 = (bf16[192,256]{1,0:T(8,128)(2,1)S(1)}, bf16[192,256]{1,0:T(8,128)(2,1)S(1)}, u32[]{:S(2)}, u32[]{:S(2)}) collective-permute-start(bf16[192,256]{1,0:T(8,128)(2,1)S(1)} %get-tuple-element.16), channel_id=1, source_target_pairs={{0,2},{1,3},{2,0},{3,1},{4,6},{5,7},{6,4},{7,5},{8,10},{9,11},{10,... | collective-permute-start | bytes 294920 | tf_op jit(solution)/shard_map/ppermute | solution.py:533
  9.6 5.3 %collective-permute-start.5 = (bf16[208,256]{1,0:T(8,128)(2,1)S(1)}, bf16[208,256]{1,0:T(8,128)(2,1)S(1)}, u32[]{:S(2)}, u32[]{:S(2)}) collective-permute-start(bf16[208,256]{1,0:T(8,128)(2,1)S(1)} %get-tuple-element.18), channel_id=1, source_target_pairs={{0,1},{1,0},{2,3},{3,2},{4,5},{5,4},{6,7},{7,6},{8,9},{9,8},{10,11... | collective-permute-start | bytes 319496 | tf_op jit(solution)/shard_map/ppermute | solution.py:533
  9.6 5.3 %collective-permute-start.4 = (bf16[192,256]{1,0:T(8,128)(2,1)S(1)}, bf16[192,256]{1,0:T(8,128)(2,1)S(1)}, u32[]{:S(2)}, u32[]{:S(2)}) collective-permute-start(bf16[192,256]{1,0:T(8,128)(2,1)S(1)} %get-tuple-element.17), channel_id=1, source_target_pairs={{0,3},{1,2},{2,1},{3,0},{4,7},{5,6},{6,5},{7,4},{8,11},{9,10},{10,... | collective-permute-start | bytes 294920 | tf_op jit(solution)/shard_map/ppermute | solution.py:533
  9.8 6.9 %collective-permute-start = (bf16[128,256]{1,0:T(8,128)(2,1)S(1)}, bf16[128,256]{1,0:T(8,128)(2,1)S(1)}, u32[]{:S(2)}, u32[]{:S(2)}) collective-permute-start(bf16[128,256]{1,0:T(8,128)(2,1)S(1)} %get-tuple-element.13), channel_id=1, source_target_pairs={{0,2},{1,3},{2,0},{3,1},{4,6},{5,7},{6,4},{7,5},{8,10},{9,11},{10,... | collective-permute-start | bytes 196616 | tf_op jit(solution)/shard_map/ppermute | solution.py:533
  11.7 5.1 %collective-permute-start.1 = (bf16[128,256]{1,0:T(8,128)(2,1)S(1)}, bf16[128,256]{1,0:T(8,128)(2,1)S(1)}, u32[]{:S(2)}, u32[]{:S(2)}) collective-permute-start(bf16[128,256]{1,0:T(8,128)(2,1)S(1)} %get-tuple-element.14), channel_id=1, source_target_pairs={{0,3},{1,2},{2,1},{3,0},{4,7},{5,6},{6,5},{7,4},{8,11},{9,10},{10,... | collective-permute-start | bytes 196616 | tf_op jit(solution)/shard_map/ppermute | solution.py:533
  12.8 4.1 %collective-permute-start.2 = (bf16[128,256]{1,0:T(8,128)(2,1)S(1)}, bf16[128,256]{1,0:T(8,128)(2,1)S(1)}, u32[]{:S(2)}, u32[]{:S(2)}) collective-permute-start(bf16[128,256]{1,0:T(8,128)(2,1)S(1)} %get-tuple-element.15), channel_id=1, source_target_pairs={{0,1},{1,0},{2,3},{3,2},{4,5},{5,4},{6,7},{7,6},{8,9},{9,8},{10,11... | collective-permute-start | bytes 196616 | tf_op jit(solution)/shard_map/ppermute | solution.py:533
  15.1 5.5 %collective-permute-start.9 = (bf16[6,16,640]{2,1,0:T(8,128)(2,1)S(1)}, bf16[6,16,640]{2,1,0:T(8,128)(2,1)S(1)}, u32[]{:S(2)}, u32[]{:S(2)}) collective-permute-start(bf16[6,16,640]{2,1,0:T(8,128)(2,1)S(1)} %spill_4.1), channel_id=1, source_target_pairs={{0,4},{4,0},{8,12},{12,8},{1,5},{5,1},{9,13},{13,9},{2,6},{6,2},{1... | collective-permute-start | bytes 368648 | tf_op jit(solution)/shard_map/ppermute | solution.py:570
  16.7 3.9 %collective-permute-start.8 = (bf16[6,16,640]{2,1,0:T(8,128)(2,1)S(1)}, bf16[6,16,640]{2,1,0:T(8,128)(2,1)S(1)}, u32[]{:S(2)}, u32[]{:S(2)}) collective-permute-start(bf16[6,16,640]{2,1,0:T(8,128)(2,1)S(1)} %spill_4.1), channel_id=1, source_target_pairs={{0,1},{1,0},{2,3},{3,2},{4,8},{5,9},{6,10},{7,11},{8,4},{9,5},{10,... | collective-permute-start | bytes 368648 | tf_op jit(solution)/shard_map/ppermute | solution.py:569
  17.0 5.5 %collective-permute-start.7 = (bf16[4,16,640]{2,1,0:T(8,128)(2,1)S(1)}, bf16[4,16,640]{2,1,0:T(8,128)(2,1)S(1)}, u32[]{:S(2)}, u32[]{:S(2)}) collective-permute-start(bf16[4,16,640]{2,1,0:T(8,128)(2,1)S(1)} %spill_0.1), channel_id=1, source_target_pairs={{0,4},{4,0},{8,12},{12,8},{1,5},{5,1},{9,13},{13,9},{2,6},{6,2},{1... | collective-permute-start | bytes 245768 | tf_op jit(solution)/shard_map/ppermute | solution.py:570
  20.1 2.4 %collective-permute-start.6 = (bf16[4,16,640]{2,1,0:T(8,128)(2,1)S(1)}, bf16[4,16,640]{2,1,0:T(8,128)(2,1)S(1)}, u32[]{:S(2)}, u32[]{:S(2)}) collective-permute-start(bf16[4,16,640]{2,1,0:T(8,128)(2,1)S(1)} %spill_0.1), channel_id=1, source_target_pairs={{0,1},{1,0},{2,3},{3,2},{4,8},{5,9},{6,10},{7,11},{8,4},{9,5},{10,... | collective-permute-start | bytes 245768 | tf_op jit(solution)/shard_map/ppermute | solution.py:569

commit v3 on v2

--- a/solution.py
+++ b/solution.py
@@ -103,7 +103,7 @@
     return jnp.dot(jnp.concatenate(view, axis=1), band, preferred_element_type=f32)
 
 
-def join_pair(even, odd, low, across, edge):
+def join_pair(even, odd, low, edge):
     if odd is None:
         here = jnp.where(low, even[:, :128], 0.0)
         before = jnp.where(low, 0.0, even[:, :128])
@@ -112,14 +112,18 @@
         here = jnp.where(low, even[:, :128], odd[:, :128])
         before = jnp.where(low, odd[:, :128], even[:, :128])
         after = even[:, 128:] + odd[:, 128:]
-    return join_across(pltpu.roll(before, 64, 1), here, after, across, edge)
-
-
-def join_across(before, here, after, across, edge):
+    return join_across(pltpu.roll(before, 64, 1), here, after, edge)
+
+
+def join_across(before, here, after, edge):
     rows = here.shape[0]
-    before = jnp.where(across == 0, 0.0, pltpu.roll(before, 1, 0))
-    after = jnp.where(across == edge - 1, 0.0, pltpu.roll(after, rows - 1, 0))
-    return here + before + after
+    row = iota((edge, 128), 0)
+    inside = [(row != 0).astype(f32), (row != edge - 1).astype(f32)]
+    sides = [pltpu.roll(before, 1, 0), pltpu.roll(after, rows - 1, 0)]
+    lines = here.reshape(rows // edge, edge, 128)
+    for side, keep in zip(sides, inside):
+        lines = lines + side.reshape(rows // edge, edge, 128) * keep[None]
+    return lines.reshape(rows, 128)
 
 
 def folded(row, width):
@@ -153,10 +157,10 @@
         variance = folded(self.second, self.width) * (1.0 / self.voxels) - off * off
         self.center = self.base + off
         self.factor = lax.rsqrt(jnp.maximum(variance, 0.0) + epsilon) * gain
-        self.shift = shift
+        self.shift = shift - self.center * self.factor
 
     def give(self, block, mask):
-        scaled = (block - self.center) * self.factor + self.shift
+        scaled = block * self.factor + self.shift
         scaled = jnp.maximum(scaled, leak_slope * scaled)
         return scaled if mask is None else jnp.where(mask, scaled, 0.0)
 
@@ -250,7 +254,6 @@
     source = iota((chunk * edge, area), 1)
     turn = (row % edge - source // edge) & (edge - 1)
     code = turn + edge * (source % edge - row // edge)
-    across = iota((count, 128), 0) % edge
     tile_index = lax.axis_index("tiles")
     sub_index = lax.axis_index("sub")
     position = lax.axis_index("folds") * lax.axis_size("sub") + sub_index
@@ -306,7 +309,7 @@
         odd = None
         if pair < pairs - 1:
             odd = banded(pad_one, [256 * pair + 128], count, edge, band_one[1])
-        block = join_pair(even, odd, low, across, edge)
+        block = join_pair(even, odd, low, edge)
         hidden[:, pair * 128 : (pair + 1) * 128] = block
         for slot, norm in enumerate(norms):
             norm.take(block[slot * stride : slot * stride + area], masks[pair], 3)
@@ -347,7 +350,7 @@
         refresh(quad + 1)
         even = banded(pad_two, [128 * quad], count, edge, band_two[0])
         odd = banded(pad_turned, [128 * quad], count, edge, band_two[1])
-        block = join_pair(even, odd, low, across, edge)
+        block = join_pair(even, odd, low, edge)
         outcome[:, quad * 128 : (quad + 1) * 128] = block
         for slot, norm in enumerate(seconds):
             norm.take(block[slot * stride : slot * stride + area], None, 4)

time: 23.4 us -> 23.3 us (level)
  no operation moved by 1% of the time
where the time goes in v3:
time: 23.3 us; the launch traced here: 23.1 us
  starting transfers between devices  9.86 us (42%)
  Pallas kernels  8.51 us (37%)
  waiting for transfers between devices  4.74 us (20%)
    pallas_call x1, Pallas kernels, on_device(): pl.pallas_call(functools.partial(section_kernel, (slots, edge, chunk, par...  6.51 us
    ppermute x6, starting transfers between devices, on_device(): lax.ppermute(piece, ('folds', 'sub'), pairs)  5.16 us
    ppermute x2, starting transfers between devices, on_device(): from_below.append(lax.ppermute(spill, 'tiles', even))  4.7 us
    ppermute x6, waiting for transfers between devices, on_device(): lax.ppermute(piece, ('folds', 'sub'), pairs)  3.32 us
    pallas_call x2, Pallas kernels, on_device(): pl.pallas_call(functools.partial(join_kernel, low_row), out_shape=jax.Sha...  1.47 us
    ppermute x2, waiting for transfers between devices, on_device(): from_below.append(lax.ppermute(spill, 'tiles', even))  1.41 us
    pallas_call x3, Pallas kernels, gather(): pl.pallas_call(functools.partial(gather_kernel, (slots, edge, chunk, [par...  0.53 us
  transfers between devices with their start and end apart: 10, of which 5 were waited for; matrix products, arithmetic and copies ran while one was open for 0% of the time, Pallas kernels for 6%

profile of v3, /device:TPU:0, one launch (start us, length us, event | category | flops | bytes accessed | tf_op | source)
XLA Modules:
  0.0 23.1 jit_solution(3963165018107506708)
XLA Ops:
  0.0 6.5 %section.1 = (bf16[336,256]{1,0:T(8,128)(2,1)S(1)}, bf16[128,256]{1,0:T(8,128)(2,1)S(1)}, bf16[128,256]{1,0:T(8,128)(2,1)S(1)}, bf16[128,256]{1,0:T(8,128)(2,1)S...) custom-call(s32[2,3]{1,0:T(2,128)} %corners_hbm.1, ...), custom_call_target="tpu_custom_call" | custom-call | tf_op jit(solution)/shard_map/section/pallas_call | solution.py:492
  6.5 3.0 %collective-permute-start.3 = (bf16[192,256]{1,0:T(8,128)(2,1)S(1)}, bf16[192,256]{1,0:T(8,128)(2,1)S(1)}, u32[]{:S(2)}, u32[]{:S(2)}) collective-permute-start(bf16[192,256]{1,0:T(8,128)(2,1)S(1)} %get-tuple-element.16), channel_id=1, source_target_pairs={{0,2},{1,3},{2,0},{3,1},{4,6},{5,7},{6,4},{7,5},{8,10},{9,11},{10,... | collective-permute-start | bytes 294920 | tf_op jit(solution)/shard_map/ppermute | solution.py:536
  9.5 0.0 collective-permute-start.5
  9.5 0.2 collective-permute-start.4
  9.7 1.9 %collective-permute-start = (bf16[128,256]{1,0:T(8,128)(2,1)S(1)}, bf16[128,256]{1,0:T(8,128)(2,1)S(1)}, u32[]{:S(2)}, u32[]{:S(2)}) collective-permute-start(bf16[128,256]{1,0:T(8,128)(2,1)S(1)} %get-tuple-element.13), channel_id=1, source_target_pairs={{0,2},{1,3},{2,0},{3,1},{4,6},{5,7},{6,4},{7,5},{8,10},{9,11},{10,... | collective-permute-start | bytes 196616 | tf_op jit(solution)/shard_map/ppermute | solution.py:536
  11.7 0.0 collective-permute-start.1
  11.7 1.1 %collective-permute-done.3.rest_4_.rest_1_ = bf16[192,256]{1,0:T(8,128)(2,1)S(1)} collective-permute-done((bf16[192,256]{1,0:T(8,128)(2,1)S(1)}, bf16[192,256]{1,0:T(8,128)(2,1)S(1)}, u32[]{:S(2)}, u32[]{:S(2)}) %collective-permute-start.3) | collective-permute-done | bytes 98336 | tf_op jit(solution)/shard_map/ppermute | solution.py:536
  12.7 0.0 collective-permute-start.2
  12.7 2.1 %collective-permute-done.4.rest_5_.rest_2_ = bf16[192,256]{1,0:T(8,128)(2,1)S(1)} collective-permute-done((bf16[192,256]{1,0:T(8,128)(2,1)S(1)}, bf16[192,256]{1,0:T(8,128)(2,1)S(1)}, u32[]{:S(2)}, u32[]{:S(2)}) %collective-permute-start.4) | collective-permute-done | bytes 98336 | tf_op jit(solution)/shard_map/ppermute | solution.py:536
  14.8 0.0 collective-permute-done.5.rest_6_.rest_4_.rest_3_
  14.8 0.2 spill_4.1
  15.0 1.6 %collective-permute-start.9 = (bf16[6,16,640]{2,1,0:T(8,128)(2,1)S(1)}, bf16[6,16,640]{2,1,0:T(8,128)(2,1)S(1)}, u32[]{:S(2)}, u32[]{:S(2)}) collective-permute-start(bf16[6,16,640]{2,1,0:T(8,128)(2,1)S(1)} %spill_4.1), channel_id=1, source_target_pairs={{0,4},{4,0},{8,12},{12,8},{1,5},{5,1},{9,13},{13,9},{2,6},{6,2},{1... | collective-permute-start | bytes 368648 | tf_op jit(solution)/shard_map/ppermute | solution.py:573
  16.6 0.0 collective-permute-start.8
  16.6 0.0 collective-permute-done.rest_1_
  16.7 0.1 collective-permute-done.1.rest_2_
  16.8 0.1 spill_0.1
  16.9 3.1 %collective-permute-start.7 = (bf16[4,16,640]{2,1,0:T(8,128)(2,1)S(1)}, bf16[4,16,640]{2,1,0:T(8,128)(2,1)S(1)}, u32[]{:S(2)}, u32[]{:S(2)}) collective-permute-start(bf16[4,16,640]{2,1,0:T(8,128)(2,1)S(1)} %spill_0.1), channel_id=1, source_target_pairs={{0,4},{4,0},{8,12},{12,8},{1,5},{5,1},{9,13},{13,9},{2,6},{6,2},{1... | collective-permute-start | bytes 245768 | tf_op jit(solution)/shard_map/ppermute | solution.py:573
  20.0 0.2 %own.1.own_ref = f32[10,16,640]{2,1,0:T(8,128)S(1)} custom-call(bf16[336,256]{1,0:T(8,128)(2,1)S(1)} %get-tuple-element.12.rest_0_, bf16[128,256]{1,0:T(8,128)(2,1)S(1)} %collective-permute-done.rest_1_, bf16[128,256]{1,0:T(8,128)(2,1)S(1)} %collective-permute-done.1.rest_2_, bf16[128,256]{1,0:T(8,128)(2,1)S(1)} %collective-permute-done.2.rest_3_, ...), custom_call_target="tpu_custom_call" | custom-call | flops 500000000 | bytes 2000000 | tf_op jit(solution)/shard_map/own/pallas_call | solution.py:544
  20.2 0.3 %collective-permute-done.9.even_ref = bf16[6,16,640]{2,1,0:T(8,128)(2,1)S(1)} collective-permute-done((bf16[6,16,640]{2,1,0:T(8,128)(2,1)S(1)}, bf16[6,16,640]{2,1,0:T(8,128)(2,1)S(1)}, u32[]{:S(2)}, u32[]{:S(2)}) %collective-permute-start.9) | collective-permute-done | bytes 122912 | tf_op jit(solution)/shard_map/ppermute | solution.py:573
  20.6 0.0 collective-permute-done.8.odd_ref
  20.6 0.8 %join_4.1.rest_0_ = f32[10,16,640]{2,1,0:T(8,128)} custom-call(f32[10,16,640]{2,1,0:T(8,128)S(1)} %own.1.own_ref, bf16[6,16,640]{2,1,0:T(8,128)(2,1)S(1)} %collective-permute-done.8.odd_ref, bf16[6,16,640]{2,1,0:T(8,128)(2,1)S(1)} %collective-permute-done.9.even_ref), custom_call_target="tpu_custom_call" | custom-call | tf_op jit(solution)/shard_map/join_4/pallas_call | solution.py:578
  21.3 1.1 %collective-permute-done.7.even_ref = bf16[4,16,640]{2,1,0:T(8,128)(2,1)S(1)} collective-permute-done((bf16[4,16,640]{2,1,0:T(8,128)(2,1)S(1)}, bf16[4,16,640]{2,1,0:T(8,128)(2,1)S(1)}, u32[]{:S(2)}, u32[]{:S(2)}) %collective-permute-start.7) | collective-permute-done | bytes 81952 | tf_op jit(solution)/shard_map/ppermute | solution.py:573
  22.4 0.0 collective-permute-done.6.odd_ref
  22.4 0.7 %join_0.1 = f32[10,16,640]{2,1,0:T(8,128)} custom-call(f32[10,16,640]{2,1,0:T(8,128)S(1)} %own.1.own_ref, bf16[4,16,640]{2,1,0:T(8,128)(2,1)S(1)} %collective-permute-done.6.odd_ref, bf16[4,16,640]{2,1,0:T(8,128)(2,1)S(1)} %collective-permute-done.7.even_ref, f32[10,16,640]{2,1,0:T(8,128)} %join_4.1.rest_0_), custom_call_target="tpu_custom_call", output_to_operand_aliasing={{}: (3, {})} | custom-call | tf_op jit(solution)/shard_map/join_0/pallas_call | solution.py:578
  (2 shorter events, 0.0 us)
Async XLA Ops:
  6.5 6.2 %collective-permute-start.3 = (bf16[192,256]{1,0:T(8,128)(2,1)S(1)}, bf16[192,256]{1,0:T(8,128)(2,1)S(1)}, u32[]{:S(2)}, u32[]{:S(2)}) collective-permute-start(bf16[192,256]{1,0:T(8,128)(2,1)S(1)} %get-tuple-element.16), channel_id=1, source_target_pairs={{0,2},{1,3},{2,0},{3,1},{4,6},{5,7},{6,4},{7,5},{8,10},{9,11},{10,... | collective-permute-start | bytes 294920 | tf_op jit(solution)/shard_map/ppermute | solution.py:536
  9.5 5.3 %collective-permute-start.5 = (bf16[208,256]{1,0:T(8,128)(2,1)S(1)}, bf16[208,256]{1,0:T(8,128)(2,1)S(1)}, u32[]{:S(2)}, u32[]{:S(2)}) collective-permute-start(bf16[208,256]{1,0:T(8,128)(2,1)S(1)} %get-tuple-element.18), channel_id=1, source_target_pairs={{0,1},{1,0},{2,3},{3,2},{4,5},{5,4},{6,7},{7,6},{8,9},{9,8},{10,11... | collective-permute-start | bytes 319496 | tf_op jit(solution)/shard_map/ppermute | solution.py:536
  9.5 5.3 %collective-permute-start.4 = (bf16[192,256]{1,0:T(8,128)(2,1)S(1)}, bf16[192,256]{1,0:T(8,128)(2,1)S(1)}, u32[]{:S(2)}, u32[]{:S(2)}) collective-permute-start(bf16[192,256]{1,0:T(8,128)(2,1)S(1)} %get-tuple-element.17), channel_id=1, source_target_pairs={{0,3},{1,2},{2,1},{3,0},{4,7},{5,6},{6,5},{7,4},{8,11},{9,10},{10,... | collective-permute-start | bytes 294920 | tf_op jit(solution)/shard_map/ppermute | solution.py:536
  9.7 6.9 %collective-permute-start = (bf16[128,256]{1,0:T(8,128)(2,1)S(1)}, bf16[128,256]{1,0:T(8,128)(2,1)S(1)}, u32[]{:S(2)}, u32[]{:S(2)}) collective-permute-start(bf16[128,256]{1,0:T(8,128)(2,1)S(1)} %get-tuple-element.13), channel_id=1, source_target_pairs={{0,2},{1,3},{2,0},{3,1},{4,6},{5,7},{6,4},{7,5},{8,10},{9,11},{10,... | collective-permute-start | bytes 196616 | tf_op jit(solution)/shard_map/ppermute | solution.py:536
  11.7 5.1 %collective-permute-start.1 = (bf16[128,256]{1,0:T(8,128)(2,1)S(1)}, bf16[128,256]{1,0:T(8,128)(2,1)S(1)}, u32[]{:S(2)}, u32[]{:S(2)}) collective-permute-start(bf16[128,256]{1,0:T(8,128)(2,1)S(1)} %get-tuple-element.14), channel_id=1, source_target_pairs={{0,3},{1,2},{2,1},{3,0},{4,7},{5,6},{6,5},{7,4},{8,11},{9,10},{10,... | collective-permute-start | bytes 196616 | tf_op jit(solution)/shard_map/ppermute | solution.py:536
  12.7 4.1 %collective-permute-start.2 = (bf16[128,256]{1,0:T(8,128)(2,1)S(1)}, bf16[128,256]{1,0:T(8,128)(2,1)S(1)}, u32[]{:S(2)}, u32[]{:S(2)}) collective-permute-start(bf16[128,256]{1,0:T(8,128)(2,1)S(1)} %get-tuple-element.15), channel_id=1, source_target_pairs={{0,1},{1,0},{2,3},{3,2},{4,5},{5,4},{6,7},{7,6},{8,9},{9,8},{10,11... | collective-permute-start | bytes 196616 | tf_op jit(solution)/shard_map/ppermute | solution.py:536
  15.0 5.5 %collective-permute-start.9 = (bf16[6,16,640]{2,1,0:T(8,128)(2,1)S(1)}, bf16[6,16,640]{2,1,0:T(8,128)(2,1)S(1)}, u32[]{:S(2)}, u32[]{:S(2)}) collective-permute-start(bf16[6,16,640]{2,1,0:T(8,128)(2,1)S(1)} %spill_4.1), channel_id=1, source_target_pairs={{0,4},{4,0},{8,12},{12,8},{1,5},{5,1},{9,13},{13,9},{2,6},{6,2},{1... | collective-permute-start | bytes 368648 | tf_op jit(solution)/shard_map/ppermute | solution.py:573
  16.6 3.9 %collective-permute-start.8 = (bf16[6,16,640]{2,1,0:T(8,128)(2,1)S(1)}, bf16[6,16,640]{2,1,0:T(8,128)(2,1)S(1)}, u32[]{:S(2)}, u32[]{:S(2)}) collective-permute-start(bf16[6,16,640]{2,1,0:T(8,128)(2,1)S(1)} %spill_4.1), channel_id=1, source_target_pairs={{0,1},{1,0},{2,3},{3,2},{4,8},{5,9},{6,10},{7,11},{8,4},{9,5},{10,... | collective-permute-start | bytes 368648 | tf_op jit(solution)/shard_map/ppermute | solution.py:572
  16.9 5.5 %collective-permute-start.7 = (bf16[4,16,640]{2,1,0:T(8,128)(2,1)S(1)}, bf16[4,16,640]{2,1,0:T(8,128)(2,1)S(1)}, u32[]{:S(2)}, u32[]{:S(2)}) collective-permute-start(bf16[4,16,640]{2,1,0:T(8,128)(2,1)S(1)} %spill_0.1), channel_id=1, source_target_pairs={{0,4},{4,0},{8,12},{12,8},{1,5},{5,1},{9,13},{13,9},{2,6},{6,2},{1... | collective-permute-start | bytes 245768 | tf_op jit(solution)/shard_map/ppermute | solution.py:573
  20.0 2.4 %collective-permute-start.6 = (bf16[4,16,640]{2,1,0:T(8,128)(2,1)S(1)}, bf16[4,16,640]{2,1,0:T(8,128)(2,1)S(1)}, u32[]{:S(2)}, u32[]{:S(2)}) collective-permute-start(bf16[4,16,640]{2,1,0:T(8,128)(2,1)S(1)} %spill_0.1), channel_id=1, source_target_pairs={{0,1},{1,0},{2,3},{3,2},{4,8},{5,9},{6,10},{7,11},{8,4},{9,5},{10,... | collective-permute-start | bytes 245768 | tf_op jit(solution)/shard_map/ppermute | solution.py:572

commit v4 on v3

--- a/solution.py
+++ b/solution.py
@@ -477,7 +477,7 @@
     area = edge * edge
     lanes = edge * classes
     padded = slots * (area + edge) + edge
-    middle = chunk * 2 // 5
+    middle = chunk // 2
     halves = ((0, middle), (middle, chunk))
     parts = [(0, 0, chunk, True)]
     for low_row, high_row in halves:

time: 23.3 us -> 23.6 us (1.013)
  waiting for transfers between devices: 4.74 us -> 5.66 us
  starting transfers between devices: 9.86 us -> 9.14 us
    ppermute x2, starting transfers between devices: 4.7 us -> 3.64 us  [on_device(): from_below.append(lax.ppermute(spill, 'tiles', even))]
    ppermute x2, waiting for transfers between devices: 1.41 us -> 2.32 us  [on_device(): from_below.append(lax.ppermute(spill, 'tiles', even))]
    ppermute x2, starting transfers between devices: 0.01 us -> 0.34 us  [on_device(): from_below.append(lax.ppermute(spill, ('tiles', 'folds', 'sub'), odd))]
  transfers between devices with their start and end apart: 10 -> 10, of which waited for: 5 -> 6; matrix products, arithmetic and copies ran while one was open for 0% -> 0% of each run, Pallas kernels for 6% -> 5%
where the time goes in v4:
time: 23.6 us; the launch traced here: 23.4 us
  starting transfers between devices  9.14 us (39%)
  Pallas kernels  8.51 us (36%)
  waiting for transfers between devices  5.66 us (24%)
    pallas_call x1, Pallas kernels, on_device(): pl.pallas_call(functools.partial(section_kernel, (slots, edge, chunk, par...  6.51 us
    ppermute x6, starting transfers between devices, on_device(): lax.ppermute(piece, ('folds', 'sub'), pairs)  5.15 us
    ppermute x2, starting transfers between devices, on_device(): from_below.append(lax.ppermute(spill, 'tiles', even))  3.64 us
    ppermute x6, waiting for transfers between devices, on_device(): lax.ppermute(piece, ('folds', 'sub'), pairs)  3.34 us
    ppermute x2, waiting for transfers between devices, on_device(): from_below.append(lax.ppermute(spill, 'tiles', even))  2.32 us
    pallas_call x2, Pallas kernels, on_device(): pl.pallas_call(functools.partial(join_kernel, low_row), out_shape=jax.Sha...  1.47 us
    pallas_call x3, Pallas kernels, gather(): pl.pallas_call(functools.partial(gather_kernel, (slots, edge, chunk, [par...  0.53 us
  transfers between devices with their start and end apart: 10, of which 6 were waited for; matrix products, arithmetic and copies ran while one was open for 0% of the time, Pallas kernels for 5%

profile of v4, /device:TPU:0, one launch (start us, length us, event | category | flops | bytes accessed | tf_op | source)
XLA Modules:
  0.0 23.4 jit_solution(5330290985377021642)
XLA Ops:
  0.0 6.5 %section.1 = (bf16[336,256]{1,0:T(8,128)(2,1)S(1)}, bf16[160,256]{1,0:T(8,128)(2,1)S(1)}, bf16[160,256]{1,0:T(8,128)(2,1)S(1)}, bf16[160,256]{1,0:T(8,128)(2,1)S...) custom-call(s32[2,3]{1,0:T(2,128)} %corners_hbm.1, ...), custom_call_target="tpu_custom_call" | custom-call | tf_op jit(solution)/shard_map/section/pallas_call | solution.py:492
  6.5 3.0 %collective-permute-start.3 = (bf16[160,256]{1,0:T(8,128)(2,1)S(1)}, bf16[160,256]{1,0:T(8,128)(2,1)S(1)}, u32[]{:S(2)}, u32[]{:S(2)}) collective-permute-start(bf16[160,256]{1,0:T(8,128)(2,1)S(1)} %get-tuple-element.16), channel_id=1, source_target_pairs={{0,2},{1,3},{2,0},{3,1},{4,6},{5,7},{6,4},{7,5},{8,10},{9,11},{10,... | collective-permute-start | bytes 245768 | tf_op jit(solution)/shard_map/ppermute | solution.py:536
  9.5 0.0 collective-permute-start.5
  9.5 0.2 collective-permute-start.4
  9.7 1.9 %collective-permute-start = (bf16[160,256]{1,0:T(8,128)(2,1)S(1)}, bf16[160,256]{1,0:T(8,128)(2,1)S(1)}, u32[]{:S(2)}, u32[]{:S(2)}) collective-permute-start(bf16[160,256]{1,0:T(8,128)(2,1)S(1)} %get-tuple-element.13), channel_id=1, source_target_pairs={{0,2},{1,3},{2,0},{3,1},{4,6},{5,7},{6,4},{7,5},{8,10},{9,11},{10,... | collective-permute-start | bytes 245768 | tf_op jit(solution)/shard_map/ppermute | solution.py:536
  11.7 0.0 collective-permute-start.1
  11.7 0.7 %collective-permute-done.3.rest_4_.rest_1_ = bf16[160,256]{1,0:T(8,128)(2,1)S(1)} collective-permute-done((bf16[160,256]{1,0:T(8,128)(2,1)S(1)}, bf16[160,256]{1,0:T(8,128)(2,1)S(1)}, u32[]{:S(2)}, u32[]{:S(2)}) %collective-permute-start.3) | collective-permute-done | bytes 81952 | tf_op jit(solution)/shard_map/ppermute | solution.py:536
  12.4 0.0 collective-permute-start.2
  12.4 1.8 %collective-permute-done.4.rest_5_.rest_2_ = bf16[160,256]{1,0:T(8,128)(2,1)S(1)} collective-permute-done((bf16[160,256]{1,0:T(8,128)(2,1)S(1)}, bf16[160,256]{1,0:T(8,128)(2,1)S(1)}, u32[]{:S(2)}, u32[]{:S(2)}) %collective-permute-start.4) | collective-permute-done | bytes 81952 | tf_op jit(solution)/shard_map/ppermute | solution.py:536
  14.1 0.0 collective-permute-done.5.rest_6_.rest_4_.rest_3_
  14.1 0.1 spill_5.1
  14.3 1.6 %collective-permute-start.9 = (bf16[5,16,640]{2,1,0:T(8,128)(2,1)S(1)}, bf16[5,16,640]{2,1,0:T(8,128)(2,1)S(1)}, u32[]{:S(2)}, u32[]{:S(2)}) collective-permute-start(bf16[5,16,640]{2,1,0:T(8,128)(2,1)S(1)} %spill_5.1), channel_id=1, source_target_pairs={{0,4},{4,0},{8,12},{12,8},{1,5},{5,1},{9,13},{13,9},{2,6},{6,2},{1... | collective-permute-start | bytes 307208 | tf_op jit(solution)/shard_map/ppermute | solution.py:573
  15.9 0.3 %collective-permute-start.8 = (bf16[5,16,640]{2,1,0:T(8,128)(2,1)S(1)}, bf16[5,16,640]{2,1,0:T(8,128)(2,1)S(1)}, u32[]{:S(2)}, u32[]{:S(2)}) collective-permute-start(bf16[5,16,640]{2,1,0:T(8,128)(2,1)S(1)} %spill_5.1), channel_id=1, source_target_pairs={{0,1},{1,0},{2,3},{3,2},{4,8},{5,9},{6,10},{7,11},{8,4},{9,5},{10,... | collective-permute-start | bytes 307208 | tf_op jit(solution)/shard_map/ppermute | solution.py:572
  16.2 0.4 %collective-permute-done.rest_1_ = bf16[160,256]{1,0:T(8,128)(2,1)S(1)} collective-permute-done((bf16[160,256]{1,0:T(8,128)(2,1)S(1)}, bf16[160,256]{1,0:T(8,128)(2,1)S(1)}, u32[]{:S(2)}, u32[]{:S(2)}) %collective-permute-start) | collective-permute-done | bytes 81952 | tf_op jit(solution)/shard_map/ppermute | solution.py:536
  16.7 0.5 %collective-permute-done.1.rest_2_ = bf16[160,256]{1,0:T(8,128)(2,1)S(1)} collective-permute-done((bf16[160,256]{1,0:T(8,128)(2,1)S(1)}, bf16[160,256]{1,0:T(8,128)(2,1)S(1)}, u32[]{:S(2)}, u32[]{:S(2)}) %collective-permute-start.1) | collective-permute-done | bytes 81952 | tf_op jit(solution)/shard_map/ppermute | solution.py:536
  17.1 0.0 collective-permute-done.2.rest_3_
  17.1 0.1 spill_0.1
  17.3 2.0 %collective-permute-start.7 = (bf16[5,16,640]{2,1,0:T(8,128)(2,1)S(1)}, bf16[5,16,640]{2,1,0:T(8,128)(2,1)S(1)}, u32[]{:S(2)}, u32[]{:S(2)}) collective-permute-start(bf16[5,16,640]{2,1,0:T(8,128)(2,1)S(1)} %spill_0.1), channel_id=1, source_target_pairs={{0,4},{4,0},{8,12},{12,8},{1,5},{5,1},{9,13},{13,9},{2,6},{6,2},{1... | collective-permute-start | bytes 307208 | tf_op jit(solution)/shard_map/ppermute | solution.py:573
  19.3 0.2 %own.1.own_ref = f32[10,16,640]{2,1,0:T(8,128)S(1)} custom-call(bf16[336,256]{1,0:T(8,128)(2,1)S(1)} %get-tuple-element.12.rest_0_, bf16[160,256]{1,0:T(8,128)(2,1)S(1)} %collective-permute-done.rest_1_, bf16[160,256]{1,0:T(8,128)(2,1)S(1)} %collective-permute-done.1.rest_2_, bf16[160,256]{1,0:T(8,128)(2,1)S(1)} %collective-permute-done.2.rest_3_, ...), custom_call_target="tpu_custom_call" | custom-call | flops 500000000 | bytes 2000000 | tf_op jit(solution)/shard_map/own/pallas_call | solution.py:544
  19.5 0.2 collective-permute-done.9.even_ref
  19.7 0.0 collective-permute-done.8.odd_ref
  19.7 0.7 %join_5.1.rest_0_ = f32[10,16,640]{2,1,0:T(8,128)} custom-call(f32[10,16,640]{2,1,0:T(8,128)S(1)} %own.1.own_ref, bf16[5,16,640]{2,1,0:T(8,128)(2,1)S(1)} %collective-permute-done.8.odd_ref, bf16[5,16,640]{2,1,0:T(8,128)(2,1)S(1)} %collective-permute-done.9.even_ref), custom_call_target="tpu_custom_call" | custom-call | tf_op jit(solution)/shard_map/join_5/pallas_call | solution.py:578
  20.5 2.1 %collective-permute-done.7.even_ref = bf16[5,16,640]{2,1,0:T(8,128)(2,1)S(1)} collective-permute-done((bf16[5,16,640]{2,1,0:T(8,128)(2,1)S(1)}, bf16[5,16,640]{2,1,0:T(8,128)(2,1)S(1)}, u32[]{:S(2)}, u32[]{:S(2)}) %collective-permute-start.7) | collective-permute-done | bytes 102432 | tf_op jit(solution)/shard_map/ppermute | solution.py:573
  22.6 0.7 %join_0.1 = f32[10,16,640]{2,1,0:T(8,128)} custom-call(f32[10,16,640]{2,1,0:T(8,128)S(1)} %own.1.own_ref, bf16[5,16,640]{2,1,0:T(8,128)(2,1)S(1)} %collective-permute-done.6.odd_ref, bf16[5,16,640]{2,1,0:T(8,128)(2,1)S(1)} %collective-permute-done.7.even_ref, f32[10,16,640]{2,1,0:T(8,128)} %join_5.1.rest_0_), custom_call_target="tpu_custom_call", output_to_operand_aliasing={{}: (3, {})} | custom-call | tf_op jit(solution)/shard_map/join_0/pallas_call | solution.py:578
  (2 shorter events, 0.0 us)
Async XLA Ops:
  6.5 5.8 %collective-permute-start.3 = (bf16[160,256]{1,0:T(8,128)(2,1)S(1)}, bf16[160,256]{1,0:T(8,128)(2,1)S(1)}, u32[]{:S(2)}, u32[]{:S(2)}) collective-permute-start(bf16[160,256]{1,0:T(8,128)(2,1)S(1)} %get-tuple-element.16), channel_id=1, source_target_pairs={{0,2},{1,3},{2,0},{3,1},{4,6},{5,7},{6,4},{7,5},{8,10},{9,11},{10,... | collective-permute-start | bytes 245768 | tf_op jit(solution)/shard_map/ppermute | solution.py:536
  9.5 4.6 %collective-permute-start.5 = (bf16[176,256]{1,0:T(8,128)(2,1)S(1)}, bf16[176,256]{1,0:T(8,128)(2,1)S(1)}, u32[]{:S(2)}, u32[]{:S(2)}) collective-permute-start(bf16[176,256]{1,0:T(8,128)(2,1)S(1)} %get-tuple-element.18), channel_id=1, source_target_pairs={{0,1},{1,0},{2,3},{3,2},{4,5},{5,4},{6,7},{7,6},{8,9},{9,8},{10,11... | collective-permute-start | bytes 270344 | tf_op jit(solution)/shard_map/ppermute | solution.py:536
  9.5 4.6 %collective-permute-start.4 = (bf16[160,256]{1,0:T(8,128)(2,1)S(1)}, bf16[160,256]{1,0:T(8,128)(2,1)S(1)}, u32[]{:S(2)}, u32[]{:S(2)}) collective-permute-start(bf16[160,256]{1,0:T(8,128)(2,1)S(1)} %get-tuple-element.17), channel_id=1, source_target_pairs={{0,3},{1,2},{2,1},{3,0},{4,7},{5,6},{6,5},{7,4},{8,11},{9,10},{10,... | collective-permute-start | bytes 245768 | tf_op jit(solution)/shard_map/ppermute | solution.py:536
  9.7 6.9 %collective-permute-start = (bf16[160,256]{1,0:T(8,128)(2,1)S(1)}, bf16[160,256]{1,0:T(8,128)(2,1)S(1)}, u32[]{:S(2)}, u32[]{:S(2)}) collective-permute-start(bf16[160,256]{1,0:T(8,128)(2,1)S(1)} %get-tuple-element.13), channel_id=1, source_target_pairs={{0,2},{1,3},{2,0},{3,1},{4,6},{5,7},{6,4},{7,5},{8,10},{9,11},{10,... | collective-permute-start | bytes 245768 | tf_op jit(solution)/shard_map/ppermute | solution.py:536
  11.7 5.5 %collective-permute-start.1 = (bf16[160,256]{1,0:T(8,128)(2,1)S(1)}, bf16[160,256]{1,0:T(8,128)(2,1)S(1)}, u32[]{:S(2)}, u32[]{:S(2)}) collective-permute-start(bf16[160,256]{1,0:T(8,128)(2,1)S(1)} %get-tuple-element.14), channel_id=1, source_target_pairs={{0,3},{1,2},{2,1},{3,0},{4,7},{5,6},{6,5},{7,4},{8,11},{9,10},{10,... | collective-permute-start | bytes 245768 | tf_op jit(solution)/shard_map/ppermute | solution.py:536
  12.4 4.8 %collective-permute-start.2 = (bf16[160,256]{1,0:T(8,128)(2,1)S(1)}, bf16[160,256]{1,0:T(8,128)(2,1)S(1)}, u32[]{:S(2)}, u32[]{:S(2)}) collective-permute-start(bf16[160,256]{1,0:T(8,128)(2,1)S(1)} %get-tuple-element.15), channel_id=1, source_target_pairs={{0,1},{1,0},{2,3},{3,2},{4,5},{5,4},{6,7},{7,6},{8,9},{9,8},{10,11... | collective-permute-start | bytes 245768 | tf_op jit(solution)/shard_map/ppermute | solution.py:536
  14.3 5.5 %collective-permute-start.9 = (bf16[5,16,640]{2,1,0:T(8,128)(2,1)S(1)}, bf16[5,16,640]{2,1,0:T(8,128)(2,1)S(1)}, u32[]{:S(2)}, u32[]{:S(2)}) collective-permute-start(bf16[5,16,640]{2,1,0:T(8,128)(2,1)S(1)} %spill_5.1), channel_id=1, source_target_pairs={{0,4},{4,0},{8,12},{12,8},{1,5},{5,1},{9,13},{13,9},{2,6},{6,2},{1... | collective-permute-start | bytes 307208 | tf_op jit(solution)/shard_map/ppermute | solution.py:573
  15.9 3.8 %collective-permute-start.8 = (bf16[5,16,640]{2,1,0:T(8,128)(2,1)S(1)}, bf16[5,16,640]{2,1,0:T(8,128)(2,1)S(1)}, u32[]{:S(2)}, u32[]{:S(2)}) collective-permute-start(bf16[5,16,640]{2,1,0:T(8,128)(2,1)S(1)} %spill_5.1), channel_id=1, source_target_pairs={{0,1},{1,0},{2,3},{3,2},{4,8},{5,9},{6,10},{7,11},{8,4},{9,5},{10,... | collective-permute-start | bytes 307208 | tf_op jit(solution)/shard_map/ppermute | solution.py:572
  17.3 5.3 %collective-permute-start.7 = (bf16[5,16,640]{2,1,0:T(8,128)(2,1)S(1)}, bf16[5,16,640]{2,1,0:T(8,128)(2,1)S(1)}, u32[]{:S(2)}, u32[]{:S(2)}) collective-permute-start(bf16[5,16,640]{2,1,0:T(8,128)(2,1)S(1)} %spill_0.1), channel_id=1, source_target_pairs={{0,4},{4,0},{8,12},{12,8},{1,5},{5,1},{9,13},{13,9},{2,6},{6,2},{1... | collective-permute-start | bytes 307208 | tf_op jit(solution)/shard_map/ppermute | solution.py:573
  19.3 3.3 %collective-permute-start.6 = (bf16[5,16,640]{2,1,0:T(8,128)(2,1)S(1)}, bf16[5,16,640]{2,1,0:T(8,128)(2,1)S(1)}, u32[]{:S(2)}, u32[]{:S(2)}) collective-permute-start(bf16[5,16,640]{2,1,0:T(8,128)(2,1)S(1)} %spill_0.1), channel_id=1, source_target_pairs={{0,1},{1,0},{2,3},{3,2},{4,8},{5,9},{6,10},{7,11},{8,4},{9,5},{10,... | collective-permute-start | bytes 307208 | tf_op jit(solution)/shard_map/ppermute | solution.py:572
